TPU v7x, 256 devices: a whole 4x4x8 slice. The times are simulated.
256 devices in a mesh: dp: 32 (over z, y), section: 8 (over x, core).
Axes of the slice: x: 4, y: 4, z: 8, core: 2. Of those that a mesh axis runs over, the one named last changes fastest.
Arguments:
- final_hidden: bfloat16 [4, 128, 5376], P(None, 'dp', 'section'), may hold values from -64 to 64
- out_weight: bfloat16 [131072, 5376], P(('dp', 'section')), may hold values from -0.25 to 0.25
- targets: int32 [4, 128], replicated, may hold values from 0 to 131071
- token_weight: float32 [4, 128], replicated, may hold values from 0.25 to 4
Outputs:
- loss: float32 [4, 128], replicated
- grad_hidden: bfloat16 [4, 128, 5376], P(None, 'dp', 'section')
- grad_weight: bfloat16 [131072, 5376], P(('dp', 'section'))
All inputs are finite; a program needn't handle non-finite values.
Results may differ from a plain program's by a relative error of at most 0.0047.
Values may be sent and summed in bfloat16 or wider, within the bound.
A program may use at most 128 MiB of HBM per device.

v0:
```python
import jax
import jax.numpy as jnp
from jax import lax
from jax.sharding import PartitionSpec as P


def per_device(final_hidden, out_weight, targets, token_weight):
    features = lax.all_gather(final_hidden, "section", axis=2, tiled=True)
    gathered = lax.all_gather(features, "dp", axis=1, tiled=True)
    micro_count = gathered.shape[0]
    batch_rows = gathered.shape[1]
    model_width = gathered.shape[2]
    token_rows = gathered.reshape(-1, model_width)
    vocab_local = out_weight.shape[0]
    logits = lax.dot_general(
        token_rows, out_weight, (((1,), (1,)), ((), ())), preferred_element_type=jnp.float32
    )
    device_rank = lax.axis_index("dp") * lax.axis_size("section") + lax.axis_index("section")
    vocab_ids = device_rank * vocab_local + lax.broadcasted_iota(jnp.int32, (1, vocab_local), 1)
    matches = vocab_ids == targets.reshape(-1, 1)
    picked_local = jnp.sum(jnp.where(matches, logits, 0.0), axis=1)
    local_top = jnp.max(logits, axis=1)
    highest = lax.pmax(local_top, ("dp", "section"))
    local_total = jnp.sum(jnp.exp(logits - highest[:, None]), axis=1)
    summed, picked = lax.psum((local_total, picked_local), ("dp", "section"))
    log_norm = highest + jnp.log(summed)
    loss = (log_norm - picked).reshape(micro_count, batch_rows)
    logit_grads = (
        token_weight.reshape(-1, 1)
        * (jnp.exp(logits - log_norm[:, None]) - matches.astype(jnp.float32))
    ).astype(jnp.bfloat16)
    input_terms = jnp.dot(logit_grads, out_weight, preferred_element_type=jnp.float32).reshape(
        micro_count, batch_rows, model_width
    )
    token_part = lax.psum_scatter(input_terms, "dp", scatter_dimension=1, tiled=True)
    grad_total = lax.psum_scatter(token_part, "section", scatter_dimension=2, tiled=True)
    grad_hidden = grad_total.astype(jnp.bfloat16)
    grad_weight = lax.dot_general(
        logit_grads, token_rows, (((0,), (0,)), ((), ())), preferred_element_type=jnp.float32
    ).astype(jnp.bfloat16)
    return (loss, grad_hidden, grad_weight)


def solution(mesh):
    in_specs = (P(None, "dp", "section"), P(("dp", "section"), None), P(), P())
    out_specs = (P(), P(None, "dp", "section"), P(("dp", "section"), None))
    return jax.shard_map(
        per_device, mesh=mesh, in_specs=in_specs, out_specs=out_specs, check_vma=False
    )
```

profile of v0, /device:TPU:8, one launch (start us, length us, event | category | flops | bytes accessed | tf_op | source)
XLA Modules:
  0.0 604.9 jit_solution(17518032063287761229)
XLA Ops:
  7.2 0.0 all-gather.2.cloned.1.call-start
  7.2 1.2 copy.9
  8.4 28.4 %all_gather.6 = bf16[4,4,5376]{1,0,2:T(4,128)(2,1)} all-gather(bf16[4,4,672]{1,0,2:T(4,128)(2,1)S(1)} %copy.9), channel_id=1, replica_groups=mesh['dp'=32,'section'=8] {'section'}, dimensions={2}, use_global_device_ids=true | all-gather | bytes 193536 | tf_op jit(solution)/shard_map/all_gather | solution.py:8
  36.8 8.3 %copy.10 = bf16[4,4,5376]{2,0,1:T(4,128)(2,1)} copy(bf16[4,4,5376]{1,0,2:T(4,128)(2,1)} %all_gather.6) | data formatting | bytes 344064 | tf_op jit(solution)/shard_map/all_gather | solution.py:8
  45.1 0.0 all-gather.2.cloned.1.call-update
  45.1 0.0 all-reduce.4.cloned.1.call-start
  45.2 86.9 %all-gather.2.cloned.1.call-done = bf16[4,128,5376]{2,0,1:T(4,128)(2,1)} async-done(((bf16[4,4,5376]{2,0,1:T(4,128)(2,1)}), bf16[4,128,5376]{2,0,1:T(4,128)(2,1)}) %all-gather.2.cloned.1.call-update) | async-done | bytes 5505040 | tf_op jit(solution)/shard_map/all_gather | solution.py:9
  132.1 3.1 copy.11
  135.2 0.0 copy-start
  135.2 0.0 copy-start.1
  135.2 0.0 copy-start.2
  135.2 7.1 %fusion.7 = (f32[512]{0:T(512)S(1)}, f32[512,512]{0,1:T(8,128)S(1)}) fusion(bf16[512,5376]{1,0:T(8,128)(2,1)S(1)} %bitcast.17, bf16[512,5376]{1,0:T(8,128)(2,1)} %param.5), kind=kOutput, calls=%fused_computation.13 | convolution fusion | flops 2818833920 | bytes 12060672 | tf_op jit(solution)/shard_map/dot_general | solution.py:15
  142.2 0.0 copy-done
  142.3 73.7 %pmax.7 = f32[512]{0:T(512)S(1)} all-reduce(f32[512]{0:T(512)S(1)} %get-tuple-element.9), channel_id=1, replica_groups=mesh['dp'=32,'section'=8] {'dp','section'}, use_global_device_ids=true, to_apply=%region_1.2 | all-reduce | flops 512 | bytes 4096 | tf_op jit(solution)/shard_map/pmax | solution.py:23
  216.0 0.0 copy-done.1
  216.0 0.3 fusion
  216.2 73.9 %all-reduce.1 = (f32[512]{0:T(512)S(1)}, f32[512]{0:T(512)S(1)}) all-reduce(f32[512]{0:T(512)S(1)} %get-tuple-element.4, f32[512]{0:T(512)S(1)} %get-tuple-element.3), channel_id=1, replica_groups=mesh['dp'=32,'section'=8] {'dp','section'}, use_global_device_ids=true, to_apply=%region_3.4 | all-reduce | flops 1024 | bytes 8192 | tf_op jit(solution)/shard_map/psum | solution.py:25
  290.1 0.6 subtract_bitcast_fusion
  290.7 0.0 copy-done.2
  290.7 8.4 %fusion.5 = f32[512,5376]{1,0:T(8,128)} fusion(bf16[512,5376]{1,0:T(8,128)(2,1)} %param.5, f32[512,512]{0,1:T(8,128)S(1)} %get-tuple-element.10, f32[512]{0:T(512)S(1)} %get-tuple-element.8, f32[512]{0:T(512)S(1)} %bitcast.23, s32[512]{0:T(512)S(1)} %bitcast.21, s32[512]{0:T(512)S(1)} %iota_add_fusion), kind=kOutput, calls=%fused_computation.12 | convolution fusion | flops 2820145152 | bytes 17571840 | tf_op jit(solution)/shard_map/dot_general | solution.py:32
  299.1 0.0 copy-start.3
  299.1 0.0 all-reduce.4.cloned.1.call-update
  299.1 0.0 reduce-scatter.5.cloned.1.call-start
  299.2 0.6 copy-done.3
  299.8 0.6 dynamic-slice
  301.0 240.5 %all-reduce.4.cloned.1.call-done = f32[4,128,5376]{2,1,0:T(8,128)} async-done(((f32[4,128,5376]{2,1,0:T(8,128)}), f32[4,128,5376]{2,1,0:T(8,128)}) %all-reduce.4.cloned.1.call-update) | async-done | bytes 11010064
  541.5 1.2 constant_dynamic-slice_fusion
  542.7 7.6 %copy.14 = f32[4,4,5376]{1,0,2:T(4,128)} copy(f32[4,4,5376]{2,1,0:T(4,128)S(1)} %constant_dynamic-slice_fusion) | data formatting | bytes 688128
  550.3 9.4 %reshape.31 = f32[5376,16]{1,0:T(8,128)} reshape(f32[5376,4,4]{2,1,0:T(4,128)} %bitcast.15) | data formatting | bytes 688128
  559.6 0.0 reduce-scatter.5.cloned.1.call-update
  559.6 7.6 %convolution_convert_fusion = bf16[512,5376]{1,0:T(8,128)(2,1)} fusion(bf16[512,5376]{1,0:T(8,128)(2,1)} %bitcast.18, f32[512,512]{0,1:T(8,128)S(1)} %get-tuple-element.10, f32[512]{0:T(512)S(1)} %get-tuple-element.8, f32[512]{0:T(512)S(1)} %bitcast.24, s32[512]{0:T(512)S(1)} %bitcast.22, s32[512]{0:T(512)S(1)} %iota_add_fusion), kind=kOutput, calls=%fused_computation | convolution fusion | flops 2822897664 | bytes 12066816 | tf_op jit(solution)/shard_map/dot_general | solution.py:38
  567.2 28.8 %reduce-scatter.5.cloned.1.call-done = f32[672,16]{1,0:T(8,128)} async-done(((f32[5376,16]{1,0:T(8,128)}), f32[672,16]{1,0:T(8,128)}) %reduce-scatter.5.cloned.1.call-update) | async-done | bytes 43024
  596.0 1.4 reshape.32
  597.3 1.1 copy.15
  (1 shorter events, 0.0 us)
Async XLA Ops:
  7.2 124.9 %all-gather.2.cloned.1.call-start = ((), (), s32[]{:S(2)}) async-start(), calls=%async_computation.1 | async-start | bytes 5677056 | tf_op jit(solution)/shard_map/all_gather | solution.py:9
  45.1 496.4 %all-reduce.4.cloned.1.call-start = ((), (), s32[]{:S(2)}) async-start(), calls=%async_computation.3 | async-start | bytes 22020096
  135.2 7.1 %copy-start = (bf16[4,128,5376]{2,1,0:T(8,128)(2,1)}, bf16[4,128,5376]{2,1,0:T(8,128)(2,1)S(1)}, u32[]{:S(2)}) copy-start(bf16[4,128,5376]{2,1,0:T(8,128)(2,1)S(1)} %copy.11) | copy-start | bytes 16515076
  135.2 80.8 %copy-start.1 = (s32[4,128]{1,0:T(4,128)S(1)}, s32[4,128]{1,0:T(4,128)}, u32[]{:S(2)}) copy-start(s32[4,128]{1,0:T(4,128)} %param.6) | copy-start | bytes 6148
  135.2 155.5 %copy-start.2 = (f32[4,128]{1,0:T(4,128)S(1)}, f32[4,128]{1,0:T(4,128)}, u32[]{:S(2)}) copy-start(f32[4,128]{1,0:T(4,128)} %param.7) | copy-start | bytes 6148
  299.1 0.7 copy-start.3
  299.1 296.9 %reduce-scatter.5.cloned.1.call-start = ((), (), s32[]{:S(2)}) async-start(), calls=%async_computation.2 | async-start | bytes 3096576
Sparse Core Ops, SparseCore 0:
  45.2 86.7 all-gather.1
  299.2 242.2 all-reduce.3
  559.8 36.1 reduce-scatter.4
where the time goes:
time: 606 us; the launch traced here: 605 us
  waiting for transfers between devices  356 us (59%)
  blocking collectives  176 us (29%)
  local copies, waits for them, and re-layouts  34.2 us (6%)
  matrix products  23 us (4%)
  between operations  14.5 us (2%)
    unnamed x5, waiting for transfers between devices  269 us
    all_gather x1, waiting for transfers between devices, per_device(): gathered = lax.all_gather(features, 'dp', axis=1, tiled=True)  86.9 us
    psum x1, blocking collectives, per_device(): summed, picked = lax.psum((local_total, picked_local), ('dp', 'section'))  73.9 us
    pmax x1, blocking collectives, per_device(): highest = lax.pmax(local_top, ('dp', 'section'))  73.7 us
    all_gather x1, blocking collectives, per_device(): features = lax.all_gather(final_hidden, 'section', axis=2, tiled=True)  28.4 us
    unnamed x15, local copies, waits for them, and re-layouts  22.8 us
  transfers between devices with their start and end apart: 3, of which 3 were waited for; matrix products, arithmetic and copies ran while one was open for 1% of the time, Pallas kernels for 0%

commit v1 on v0

v1 whole, which is shorter than its diff:
```python
import functools

import jax
import jax.numpy as jnp
from jax import lax
from jax.experimental import pallas as pl
from jax.experimental.pallas import tpu as pltpu
from jax.sharding import PartitionSpec as P

MESH = pl.DeviceIdType.MESH
F32, BF16 = jnp.float32, jnp.bfloat16
NX, NY, NZ = 4, 4, 8
FRAME = 768
L0, L1, L2 = 384, 256, 128
OFF0, OFF1, OFF2 = 0, L0, L0 + L1


def frame_tile(section):
    return (21 * section) // 4


def kernel(
    h_ref, w_hbm, tgt_ref, tw_ref,
    loss_ref, gh_ref, gw_hbm,
    w, h, lt, p, pt, gw, pad, mine,
    a0, a1, a2,
    gs, rc, s0, s1, s2, r0, r1, r2, t0, t1, t2, q0, q1, q2, c0, c1, c2, d0, d1, d2,
    st1, st2,
    w_sem, gw_sem,
    ag_s, ag_r, f0_s, f0_r, f1_s, f1_r, f2_s, f2_r, st_s, st_r,
    gc_s, gc_r, rs_s, rs_r,
):
    dp = lax.axis_index("dp")
    section = lax.axis_index("section")
    z, y = dp // NY, dp % NY
    x, c = section // 2, section % 2

    def at(dz=0, dy=0, dx=0, dc=0):
        return (
            lax.rem(z + dz, NZ) * NY + lax.rem(y + dy, NY),
            lax.rem(x + dx, NX) * 2 + lax.rem(c + dc, 2),
        )

    sibling = at(dc=1)

    load_w = pltpu.make_async_copy(w_hbm, w, w_sem)
    load_w.start()

    plane = [(k // NX, k % NX) for k in range(1, NX * NY)]
    column = [(k // 2, k % 2) for k in range(1, NZ * 2)]
    barrier = pltpu.get_barrier_semaphore()
    for dy, dx in plane:
        pl.semaphore_signal(barrier, inc=1, device_id=at(dy=dy, dx=dx), device_id_type=MESH)
    for dz, dc in column:
        pl.semaphore_signal(barrier, inc=1, device_id=at(dz=dz, dc=dc), device_id_type=MESH)

    pad[...] = jnp.zeros_like(pad)
    for m in range(4):
        pad[4 * m : 4 * m + 4, 0:672] = h_ref[m].astype(F32)
    shift = lax.rem(section, 4) * 32
    framed = pltpu.roll(pad[...], shift, axis=1).astype(BF16)
    a0[c, x, z, y] = framed[:, OFF0 : OFF0 + L0]
    a1[c, x, z, y] = framed[:, OFF1 : OFF1 + L1]
    a2[c, x, z, y] = framed[:, OFF2 : OFF2 + L2]

    pl.semaphore_wait(barrier, len(plane) + len(column))

    sends = []

    def send(src, dst, s_sem, r_sem, device):
        copy = pltpu.make_async_remote_copy(
            src_ref=src, dst_ref=dst, send_sem=s_sem, recv_sem=r_sem,
            device_id=device, device_id_type=MESH,
        )
        copy.start()
        sends.append(copy)
        return copy

    slot = iter(range(1000))

    def gather(ref, axis, n):
        out = []
        for o in range(1, n):
            k = next(slot)
            out.append(send(ref, ref, ag_s.at[k], ag_r.at[k], at(**{"d" + axis: o})))
        return out

    def arrive(copies):
        for copy in copies:
            copy.wait_recv()

    e0 = gather(a0.at[c, x, z, y], "z", NZ)
    e1 = gather(a1.at[c, x, z, y], "z", NZ)
    e2 = gather(a2.at[c, x, z, y], "x", NX)
    arrive(e2)
    e2 = gather(a2.at[c, :, z, y], "y", NY)
    arrive(e0)
    e0 = gather(a0.at[c, x, :, y], "y", NY)
    arrive(e1)
    e1 = gather(a1.at[c, x, :, y], "x", NX)
    arrive(e2)
    e2 = gather(a2.at[c, :, z], "z", NZ)
    send(a2.at[c, :, z], a2.at[c, :, z], f2_s.at[0], f2_r.at[0], sibling)
    arrive(e0)
    e0 = gather(a0.at[c, x], "x", NX)
    send(a0.at[c, x], a0.at[c, x], f0_s.at[0], f0_r.at[0], sibling)
    arrive(e1)
    e1 = gather(a1.at[c, :, :, y], "y", NY)
    send(a1.at[c, :, :, y], a1.at[c, :, :, y], f1_s.at[0], f1_r.at[0], sibling)
    for o in range(1, NZ):
        e2[o - 1].wait_recv()
        part = a2.at[c, :, lax.rem(z + NZ - o, NZ)]
        send(part, part, f2_s.at[o], f2_r.at[o], sibling)
    for o in range(1, NY):
        e1[o - 1].wait_recv()
        part = a1.at[c, :, :, lax.rem(y + NY - o, NY)]
        send(part, part, f1_s.at[o], f1_r.at[o], sibling)
    for o in range(1, NX):
        e0[o - 1].wait_recv()
        part = a0.at[c, lax.rem(x + NX - o, NX)]
        send(part, part, f0_s.at[o], f0_r.at[o], sibling)

    def landed(ref, s_sem, r_sem):
        pltpu.make_async_remote_copy(
            src_ref=ref, dst_ref=ref, send_sem=s_sem, recv_sem=r_sem,
            device_id=sibling, device_id_type=MESH,
        ).wait_recv()

    other = 1 - c
    for o in range(NZ):
        landed(a2.at[other, :, lax.rem(z + NZ - o, NZ)], f2_s.at[o], f2_r.at[o])
    for o in range(NY):
        landed(a1.at[other, :, :, lax.rem(y + NY - o, NY)], f1_s.at[o], f1_r.at[o])
    for o in range(NX):
        landed(a0.at[other, lax.rem(x + NX - o, NX)], f0_s.at[o], f0_r.at[o])

    def frame_part(s, tile, zz):
        lane = tile * 128
        for buf, off, width in ((a0, OFF0, L0), (a1, OFF1, L1), (a2, OFF2, L2)):
            if off <= lane < off + width:
                v = buf[s % 2, s // 2, zz, :, :, lane - off : lane - off + 128]
                return v.reshape(NY * 16, 128)

    def assemble(zz, carry):
        rows = pl.ds(pl.multiple_of(zz * 64, 64), 64)
        for tile in range(42):
            v = None
            for s in range(8):
                if frame_tile(s) <= tile < frame_tile(s) + 6:
                    part = frame_part(s, tile - frame_tile(s), zz)
                    v = part if v is None else v + part
            h[rows, tile * 128 : tile * 128 + 128] = v
        return carry

    lax.fori_loop(0, NZ, assemble, 0)

    load_w.wait()
    lt[...] = jnp.zeros_like(lt)

    def logits_step(k, carry):
        cols = pl.ds(pl.multiple_of(k * 768, 768), 768)
        lt[...] += lax.dot_general(
            w[:, cols], h[:, cols], (((1,), (1,)), ((), ())), preferred_element_type=F32
        )
        return carry

    lax.fori_loop(0, 7, logits_step, 0)

    first_id = (dp * (NX * 2) + section) * 512
    ids = first_id + lax.broadcasted_iota(jnp.int32, (512, 512), 0)
    logits = lt[...]
    matches = ids == tgt_ref[...]
    picked = jnp.sum(jnp.where(matches, logits, 0.0), axis=0, keepdims=True)
    top = jnp.max(logits, axis=0, keepdims=True)
    lse = top + jnp.log(jnp.sum(jnp.exp(logits - top), axis=0, keepdims=True))
    for i in range(4):
        st1[0, i : i + 1, :] = lse[:, i * 128 : i * 128 + 128]
        st1[0, 4 + i : 5 + i, :] = picked[:, i * 128 : i * 128 + 128]

    def combine(buf):
        v = buf[...]
        m = jnp.max(v[:, 0:4], axis=0)
        total = m + jnp.log(jnp.sum(jnp.exp(v[:, 0:4] - m[None]), axis=0))
        return total, jnp.sum(v[:, 4:8], axis=0)

    around = []
    for k, (dy, dx) in enumerate(plane):
        around.append(send(st1.at[0], st1.at[k + 1], st_s.at[k], st_r.at[k], at(dy=dy, dx=dx)))
    arrive(around)
    total, hit = combine(st1)
    st2[0, 0:4, :] = total
    st2[0, 4:8, :] = hit
    around = []
    for k, (dz, dc) in enumerate(column):
        around.append(
            send(st2.at[0], st2.at[k + 1], st_s.at[15 + k], st_r.at[15 + k], at(dz=dz, dc=dc))
        )
    arrive(around)
    log_norm, hit = combine(st2)
    loss_ref[...] = log_norm - hit
    norm_row = jnp.concatenate([log_norm[i : i + 1] for i in range(4)], axis=1)

    for b in range(4):
        rows = slice(b * 128, b * 128 + 128)
        hot = first_id + b * 128 + lax.broadcasted_iota(jnp.int32, (128, 512), 0) == tgt_ref[...]
        g = tw_ref[...] * (jnp.exp(lt[rows, :] - norm_row) - hot.astype(F32))
        pt[rows, :] = g.astype(BF16)
        p[:, rows] = jnp.transpose(g).astype(BF16)

    def share(s):
        cols = pl.ds(pl.multiple_of(frame_tile(s) * 128, 128), FRAME)
        return lax.dot_general(
            p[...], w[:, cols], (((1,), (0,)), ((), ())), preferred_element_type=F32
        )

    def core_copy(xx):
        return pltpu.make_async_remote_copy(
            src_ref=gs.at[xx], dst_ref=rc.at[xx], send_sem=gc_s.at[xx], recv_sem=gc_r.at[xx],
            device_id=sibling, device_id_type=MESH,
        )

    def for_sibling(xx, carry):
        gs[xx] = share(xx * 2 + other).astype(BF16)
        core_copy(xx).start()
        return carry

    lax.fori_loop(0, NX, for_sibling, 0)

    def for_me(xx, carry):
        mine[...] = share(xx * 2 + c)
        core_copy(xx).wait_recv()
        for zz in range(NZ):
            v = mine[zz * 64 : zz * 64 + 64, :] + rc[xx, zz * 64 : zz * 64 + 64, :].astype(F32)
            v = v.astype(BF16)
            s0[xx, zz] = v[:, OFF0 : OFF0 + L0].reshape(NY, 16, L0)
            for yy in range(NY):
                s1[yy, xx, zz] = v[yy * 16 : yy * 16 + 16, OFF1 : OFF1 + L1]
            s2[zz, xx] = v[:, OFF2 : OFF2 + L2].reshape(NY, 16, L2)
        return carry

    lax.fori_loop(0, NX, for_me, 0)

    def scatter(src, dst, axis, n, index):
        out = []
        for o in range(1, n):
            k = next(slot)
            out.append(
                send(
                    src.at[lax.rem(index + o, n)], dst.at[o - 1],
                    rs_s.at[k - AG_COPIES], rs_r.at[k - AG_COPIES], at(**{"d" + axis: o}),
                )
            )
        return out

    e2 = scatter(s2, r2, "z", NZ, z)
    e0 = scatter(s0, r0, "x", NX, x)
    e1 = scatter(s1, r1, "y", NY, y)

    def weight_step(k, carry):
        cols = pl.ds(pl.multiple_of(k * 768, 768), 768)
        gw[:, cols] = lax.dot_general(
            pt[...], h[:, cols], (((1,), (0,)), ((), ())), preferred_element_type=F32
        ).astype(BF16)
        return carry

    lax.fori_loop(0, 7, weight_step, 0)
    store_gw = pltpu.make_async_copy(gw, gw_hbm, gw_sem)
    store_gw.start()

    def reduced(own, got, n):
        total = own.astype(F32)
        for o in range(n - 1):
            total = total + got(o).astype(F32)
        return total

    arrive(e2)
    for xx in range(NX):
        t2[xx] = reduced(s2[z, xx], lambda o: r2[o, xx], NZ).astype(BF16)
    e2 = scatter(t2, q2, "x", NX, x)
    arrive(e1)

    def sum1(xx, carry):
        t1[xx] = reduced(s1[y, xx], lambda o: r1[o, xx], NY).astype(BF16)
        return carry

    lax.fori_loop(0, NX, sum1, 0)
    e1 = scatter(t1, q1, "x", NX, x)
    arrive(e0)

    def sum0(zz, carry):
        v = reduced(s0[x, zz], lambda o: r0[o, zz], NX).astype(BF16)
        for yy in range(NY):
            t0[yy, zz] = v[yy]
        return carry

    lax.fori_loop(0, NZ, sum0, 0)
    e0 = scatter(t0, q0, "y", NY, y)

    arrive(e2)
    c2[...] = reduced(t2[x], lambda o: q2[o], NX)
    e2 = scatter(c2, d2, "y", NY, y)
    arrive(e1)
    c1[...] = reduced(t1[x], lambda o: q1[o], NX)
    e1 = scatter(c1, d1, "z", NZ, z)
    arrive(e0)
    c0[...] = reduced(t0[y], lambda o: q0[o], NY)
    e0 = scatter(c0, d0, "z", NZ, z)
    arrive(e2)
    pad[:, OFF2 : OFF2 + L2] = reduced(c2[y], lambda o: d2[o], NY)
    arrive(e1)
    pad[:, OFF1 : OFF1 + L1] = reduced(c1[z], lambda o: d1[o], NZ)
    arrive(e0)
    pad[:, OFF0 : OFF0 + L0] = reduced(c0[z], lambda o: d0[o], NZ)
    pad[...] = pltpu.roll(pad[...], lax.rem(FRAME - shift, FRAME), axis=1)
    for m in range(4):
        gh_ref[m] = pad[4 * m : 4 * m + 4, 0:672].astype(BF16)

    for copy in sends:
        copy.wait_send()

    def sent(xx, carry):
        core_copy(xx).wait_send()
        return carry

    lax.fori_loop(0, NX, sent, 0)
    store_gw.wait()


AG_COPIES = (NZ - 1) * 3 + (NX - 1) * 3 + (NY - 1) * 3
RS_COPIES = AG_COPIES


def per_device(final_hidden, out_weight, targets, token_weight):
    def order(v):
        return v.reshape(4, 32, 4).transpose(1, 0, 2).reshape(1, 512)

    vm, dma = pltpu.VMEM, pltpu.SemaphoreType.DMA
    scratch = [
        vm((512, 5376), BF16),
        vm((512, 5376), BF16),
        vm((512, 512), F32),
        vm((512, 512), BF16),
        vm((512, 512), BF16),
        vm((512, 5376), BF16),
        vm((16, FRAME), F32),
        vm((512, FRAME), F32),
        vm((2, NX, NZ, NY, 16, L0), BF16),
        vm((2, NX, NZ, NY, 16, L1), BF16),
        vm((2, NX, NZ, NY, 16, L2), BF16),
        vm((NX, 512, FRAME), BF16),
        vm((NX, 512, FRAME), BF16),
        vm((NX, NZ, NY, 16, L0), BF16),
        vm((NY, NX, NZ, 16, L1), BF16),
        vm((NZ, NX, NY, 16, L2), BF16),
        vm((NX - 1, NZ, NY, 16, L0), BF16),
        vm((NY - 1, NX, NZ, 16, L1), BF16),
        vm((NZ - 1, NX, NY, 16, L2), BF16),
        vm((NY, NZ, 16, L0), BF16),
        vm((NX, NZ, 16, L1), BF16),
        vm((NX, NY, 16, L2), BF16),
        vm((NY - 1, NZ, 16, L0), BF16),
        vm((NX - 1, NZ, 16, L1), BF16),
        vm((NX - 1, NY, 16, L2), BF16),
        vm((NZ, 16, L0), F32),
        vm((NZ, 16, L1), F32),
        vm((NY, 16, L2), F32),
        vm((NZ - 1, 16, L0), F32),
        vm((NZ - 1, 16, L1), F32),
        vm((NY - 1, 16, L2), F32),
        vm((16, 8, 128), F32),
        vm((16, 8, 128), F32),
        dma, dma,
        dma((AG_COPIES,)), dma((AG_COPIES,)),
        dma((NX,)), dma((NX,)), dma((NY,)), dma((NY,)), dma((NZ,)), dma((NZ,)),
        dma((30,)), dma((30,)),
        dma((NX,)), dma((NX,)),
        dma((RS_COPIES,)), dma((RS_COPIES,)),
    ]
    vmem = pl.BlockSpec(memory_space=pltpu.VMEM)
    hbm = pl.BlockSpec(memory_space=pl.ANY)
    loss, grad_hidden, grad_weight = pl.pallas_call(
        kernel,
        out_shape=(
            jax.ShapeDtypeStruct((4, 128), F32),
            jax.ShapeDtypeStruct((4, 4, 672), BF16),
            jax.ShapeDtypeStruct((512, 5376), BF16),
        ),
        in_specs=[vmem, hbm, vmem, vmem],
        out_specs=(vmem, vmem, hbm),
        scratch_shapes=scratch,
        compiler_params=pltpu.CompilerParams(
            collective_id=0, has_side_effects=True, vmem_limit_bytes=60 * 2**20
        ),
        name="xent",
    )(final_hidden, out_weight, order(targets), order(token_weight))
    loss = loss.reshape(32, 4, 4).transpose(1, 0, 2).reshape(4, 128)
    return (loss, grad_hidden, grad_weight)


def solution(mesh):
    in_specs = (P(None, "dp", "section"), P(("dp", "section"), None), P(), P())
    out_specs = (P(), P(None, "dp", "section"), P(("dp", "section"), None))
    return jax.shard_map(
        per_device, mesh=mesh, in_specs=in_specs, out_specs=out_specs, check_vma=False
    )
```

time: 606 us -> 111 us (0.18)
  waiting for transfers between devices: 356 us -> 0 us
  blocking collectives: 176 us -> 0 us
  Pallas kernels: 0 us -> 98.5 us
  matrix products: 23 us -> 0 us
  local copies, waits for them, and re-layouts: 34.2 us -> 11.3 us
  between operations: 14.5 us -> 0.69 us
    unnamed x5 -> x0, waiting for transfers between devices: 269 us -> none
    pallas_call x0 -> x1, Pallas kernels: none -> 98.5 us  [per_device(): pl.pallas_call(kernel, out_shape=(jax.ShapeDtypeStruct((4, 128), F32), ja...]
    all_gather x1 -> x0, waiting for transfers between devices: 86.9 us -> none  [per_device(): gathered = lax.all_gather(features, 'dp', axis=1, tiled=True)]
    psum x1 -> x0, blocking collectives: 73.9 us -> none  [per_device(): summed, picked = lax.psum((local_total, picked_local), ('dp', 'section'))]
    pmax x1 -> x0, blocking collectives: 73.7 us -> none  [per_device(): highest = lax.pmax(local_top, ('dp', 'section'))]
    all_gather x1 -> x0, blocking collectives: 28.4 us -> none  [per_device(): features = lax.all_gather(final_hidden, 'section', axis=2, tiled=True)]
    dot_general x3 -> x0, matrix products: 23 us -> none  [the longest x1 8.38 us: per_device(): jnp.dot(logit_grads, out_weight, preferred_element_type=jnp.float32)]
    unnamed x15 -> x2, local copies, waits for them, and re-layouts: 22.8 us -> 6.71 us
  transfers between devices with their start and end apart: 3 -> 0, of which waited for: 3 -> 0; matrix products, arithmetic and copies ran while one was open for 1% -> 0% of each run, Pallas kernels for 0% -> 0%
where the time goes in v1:
time: 111 us; the launch traced here: 110 us
  Pallas kernels  98.5 us (89%)
  local copies, waits for them, and re-layouts  11.3 us (10%)
    pallas_call x1, Pallas kernels, per_device(): pl.pallas_call(kernel, out_shape=(jax.ShapeDtypeStruct((4, 128), F32), ja...  98.5 us
    unnamed x2, local copies, waits for them, and re-layouts  6.71 us
    reshape x4, local copies, waits for them, and re-layouts, order(): return v.reshape(4, 32, 4).transpose(1, 0, 2).reshape(1, 512)  2.96 us

profile of v1, /device:TPU:8, one launch (start us, length us, event | category | flops | bytes accessed | tf_op | source)
XLA Modules:
  0.0 110.5 jit_solution(11862970287099860739)
XLA Ops:
  0.6 0.8 reshape.24
  1.5 0.7 reshape.25.tgt_ref
  2.2 0.8 reshape.26
  3.0 0.7 reshape.27.tw_ref
  3.7 98.5 %xent.1 = (f32[4,128]{1,0:T(4,128)}, bf16[4,4,672]{2,1,0:T(4,128)(2,1)}, bf16[512,5376]{1,0:T(8,128)(2,1)}) custom-call(bf16[4,4,672]{2,1,0:T(4,128)(2,1)} %h_ref.1, bf16[512,5376]{1,0:T(8,128)(2,1)} %w_hbm.1, s32[1,512]{1,0:T(1,128)} %reshape.25.tgt_ref, f32[1,512]{1,0:T(1,128)} %reshape.27.tw_ref), custom_call_target="tpu_custom_call" | custom-call | tf_op jit(solution)/shard_map/xent/pallas_call | solution.py:381
  102.2 0.8 reshape.28
  103.1 0.7 reshape.29
  103.7 1.4 %copy.15 = bf16[4,4,672]{2,1,0:T(4,128)(2,1)} copy(bf16[4,4,672]{2,1,0:T(4,128)(2,1)} %get-tuple-element.13) | data formatting | bytes 43008
  105.1 5.4 %copy.16 = bf16[512,5376]{1,0:T(8,128)(2,1)} copy(bf16[512,5376]{1,0:T(8,128)(2,1)} %get-tuple-element.14) | data formatting | bytes 11010048
  (3 shorter events, 0.1 us)

commit v2 on v0

v2 whole, which is shorter than its diff:
```python
import heapq

import jax
import jax.numpy as jnp
from jax import lax
from jax.experimental import pallas as pl
from jax.experimental.pallas import tpu as pltpu
from jax.sharding import PartitionSpec as P

MESH = pl.DeviceIdType.MESH
F32, BF16 = jnp.float32, jnp.bfloat16
NX, NY, NZ = 4, 4, 8
FRAME = 768
LANES = 256
REL = (2, 1, 3, 0)
COPIES = 200


def frame_tile(section):
    return (21 * section) // 4


def run_by_time(*tasks):
    heap = []
    for k, (start, task) in enumerate(tasks):
        heapq.heappush(heap, (start, k, task))
    while heap:
        _, k, task = heapq.heappop(heap)
        try:
            heapq.heappush(heap, (next(task), k, task))
        except StopIteration:
            pass


def pieces(v):
    hi = v.astype(BF16).astype(F32)
    mid = (v - hi).astype(BF16).astype(F32)
    return hi, mid, v - hi - mid


def kernel(
    h_ref, w_hbm, tgt_ref, tw_ref,
    loss_ref, gh_ref, h, pt,
    w, lt, p, pad, mine, rows, tgt, tw,
    a0, a1, a2,
    gs, rc, s0, s1, s2, u0a, u0b, l0, m0, u1a, u1b, l1, m1, l2, m2,
    t0, t1, t2, q0, q1, q2, c0, c1, c2, d0, d1, d2,
    st1, st2,
    w_sem, send_sem, recv_sem,
):
    dp = lax.axis_index("dp")
    section = lax.axis_index("section")
    z, y = dp // NY, dp % NY
    x, c = section // 2, section % 2
    other = 1 - c

    def at(dz=0, dy=0, dx=0, dc=0):
        return (
            lax.rem(z + dz, NZ) * NY + lax.rem(y + dy, NY),
            lax.rem(x + dx, NX) * 2 + lax.rem(c + dc, 2),
        )

    def zo(o):
        return lax.rem(z + o + NZ, NZ)

    def yo(o):
        return lax.rem(y + o + NY, NY)

    def xo(o):
        return lax.rem(x + o + NX, NX)

    sibling = at(dc=1)
    x_right, x_left = at(dx=1), at(dx=3)
    y_right, y_left = at(dy=1), at(dy=3)
    z_right, z_left = at(dz=1), at(dz=7)

    load_w = pltpu.make_async_copy(w_hbm, w, w_sem)
    load_w.start()

    plane = [(k // NX, k % NX) for k in range(1, NX * NY)]
    column = [(k // 2, k % 2) for k in range(1, NZ * 2)]
    barrier = pltpu.get_barrier_semaphore()
    for dy, dx in plane:
        pl.semaphore_signal(barrier, inc=1, device_id=at(dy=dy, dx=dx), device_id_type=MESH)
    for dz, dc in column:
        pl.semaphore_signal(barrier, inc=1, device_id=at(dz=dz, dc=dc), device_id_type=MESH)

    pad[...] = jnp.zeros_like(pad)
    for m in range(4):
        pad[4 * m : 4 * m + 4, 0:672] = h_ref[m].astype(F32)
    shift = lax.rem(section, 4) * 32
    framed = pltpu.roll(pad[...], shift, axis=1).astype(BF16)
    a0[c, x, z, y] = framed[:, 0:256]
    a1[c, x, z, y] = framed[:, 256:512]
    a2[c, x, z, y] = framed[:, 512:768]

    pl.semaphore_wait(barrier, len(plane) + len(column))

    sends = []

    def send(src, dst, device):
        k = len(sends)
        copy = pltpu.make_async_remote_copy(
            src_ref=src, dst_ref=dst, send_sem=send_sem.at[k], recv_sem=recv_sem.at[k],
            device_id=device, device_id_type=MESH,
        )
        copy.start()
        sends.append(copy)
        return copy

    def arrive(copies):
        for copy in copies:
            copy.wait_recv()

    def gather(ref, axis, n):
        return [send(ref, ref, at(**{"d" + axis: o})) for o in range(1, n)]

    from_sibling = []

    def pass_on(ref):
        from_sibling.append(send(ref, ref, sibling))

    def gather0():
        e = gather(a0.at[c, x, z, y], "z", NZ)
        yield 5.0
        arrive(e)
        e = gather(a0.at[c, x, :, y], "y", NY)
        yield 9.0
        arrive(e)
        up, down = pl.ds(0, 4), pl.ds(4, 4)
        own_up, own_down = a0.at[c, x, up], a0.at[c, x, down]
        ru = send(own_up, own_up, x_right)
        ld = send(own_down, own_down, x_left)
        rd = send(own_down, own_down, x_right)
        lu = send(own_up, own_up, x_left)
        pass_on(a0.at[c, x])
        yield 13.5
        ru.wait_recv()
        part = a0.at[c, xo(-1), up]
        fu = send(part, part, x_right)
        ld.wait_recv()
        part = a0.at[c, xo(1), down]
        fd = send(part, part, x_left)
        yield 16.5
        rd.wait_recv()
        pass_on(a0.at[c, xo(-1)])
        lu.wait_recv()
        pass_on(a0.at[c, xo(1)])
        yield 19.5
        fu.wait_recv()
        pass_on(a0.at[c, xo(2), up])
        fd.wait_recv()
        pass_on(a0.at[c, xo(2), down])

    def gather1():
        e = gather(a1.at[c, x, z, y], "z", NZ)
        yield 5.1
        arrive(e)
        e = gather(a1.at[c, x, :, y], "x", NX)
        yield 9.1
        arrive(e)

        def part(o, half):
            return a1.at[c, pl.ds(2 * half, 2), :, yo(o)]

        ru = send(part(0, 0), part(0, 0), y_right)
        ld = send(part(0, 1), part(0, 1), y_left)
        rd = send(part(0, 1), part(0, 1), y_right)
        lu = send(part(0, 0), part(0, 0), y_left)
        pass_on(a1.at[c, :, :, y])
        yield 13.6
        ru.wait_recv()
        fu = send(part(-1, 0), part(-1, 0), y_right)
        ld.wait_recv()
        fd = send(part(1, 1), part(1, 1), y_left)
        yield 16.6
        rd.wait_recv()
        pass_on(a1.at[c, :, :, yo(-1)])
        lu.wait_recv()
        pass_on(a1.at[c, :, :, yo(1)])
        yield 19.6
        fu.wait_recv()
        pass_on(part(2, 0))
        fd.wait_recv()
        pass_on(part(2, 1))

    def gather2():
        e = gather(a2.at[c, x, z, y], "x", NX)
        yield 3.0
        arrive(e)
        e = gather(a2.at[c, :, z, y], "y", NY)
        yield 6.0
        arrive(e)
        right, left = [], []
        for i in range(NX):
            part = a2.at[c, i, z]
            right.append(send(part, part, z_right))
            left.append(send(part, part, z_left))
        pass_on(a2.at[c, :, z])
        for k in range(1, NZ // 2):
            for i in range(NX):
                yield 6.0 + 2.75 * k + 0.7 * i
                right[i].wait_recv()
                if k < 3 or i < 2:
                    part = a2.at[c, i, zo(-k)]
                    right[i] = send(part, part, z_right)
                left[i].wait_recv()
                if k < 3 or i >= 2:
                    part = a2.at[c, i, zo(k)]
                    left[i] = send(part, part, z_left)
            pass_on(a2.at[c, :, zo(-k)])
            pass_on(a2.at[c, :, zo(k)])
        yield 19.7
        arrive(right[:2])
        pass_on(a2.at[c, pl.ds(0, 2), zo(4)])
        arrive(left[2:])
        pass_on(a2.at[c, pl.ds(2, 2), zo(4)])

    def token_order():
        yield 1.0
        t = tgt_ref[...]
        parts = [(t & 63).astype(F32), ((t >> 6) & 63).astype(F32), (t >> 12).astype(F32)]
        parts += list(pieces(tw_ref[...]))
        for i in range(6):
            for m in range(4):
                rows[m, i : i + 1, :] = parts[i][m : m + 1, :]
        yield 1.5
        src = lax.broadcasted_iota(jnp.int32, (128, 512), 0)
        dst = lax.broadcasted_iota(jnp.int32, (128, 512), 1)
        out = jnp.zeros((8, 512), F32)
        for m in range(4):
            hot = dst == (src // 4) * 16 + m * 4 + src % 4
            out += jnp.dot(
                rows[m].astype(BF16), hot.astype(BF16), preferred_element_type=F32
            )
        number = out[0:1].astype(jnp.int32) + out[1:2].astype(jnp.int32) * 64
        tgt[...] = number + out[2:3].astype(jnp.int32) * 4096
        tw[...] = out[3:4] + out[4:5] + out[5:6]

    rows[...] = jnp.zeros_like(rows)
    run_by_time((0.0, gather0()), (0.0, gather1()), (0.0, gather2()), (1.0, token_order()))
    arrive(from_sibling)
    load_w.wait()

    for s in range(8):
        acc = None
        for j, buf in enumerate((a0, a1, a2)):
            lane = frame_tile(s) * 128 + j * LANES
            v = lax.dot_general(
                w[:, lane : lane + LANES], buf[s % 2, s // 2].reshape(512, LANES),
                (((1,), (1,)), ((), ())), preferred_element_type=F32,
            )
            acc = v if acc is None else acc + v
        if s == 0:
            lt[...] = acc
        else:
            lt[...] += acc

    first_id = (dp * (NX * 2) + section) * 512
    ids = first_id + lax.broadcasted_iota(jnp.int32, (512, 512), 0)
    logits = lt[...]
    picked = jnp.sum(jnp.where(ids == tgt[...], logits, 0.0), axis=0, keepdims=True)
    top = jnp.max(logits, axis=0, keepdims=True)
    lse = top + jnp.log(jnp.sum(jnp.exp(logits - top), axis=0, keepdims=True))
    for i in range(4):
        st1[0, i : i + 1, :] = lse[:, i * 128 : i * 128 + 128]
        st1[0, 4 + i : 5 + i, :] = picked[:, i * 128 : i * 128 + 128]

    def combine(buf):
        v = buf[...]
        m = jnp.max(v[:, 0:4], axis=0)
        total = m + jnp.log(jnp.sum(jnp.exp(v[:, 0:4] - m[None]), axis=0))
        return total, jnp.sum(v[:, 4:8], axis=0)

    def frame_part(s, tile, zz):
        buf = (a0, a1, a2)[tile // 2]
        lane = (tile % 2) * 128
        return buf[s % 2, s // 2, zz, :, :, lane : lane + 128].reshape(NY * 16, 128)

    def assemble(zz, carry):
        dst = pl.ds(pl.multiple_of(zz * 64, 64), 64)
        for tile in range(42):
            v = None
            for s in range(8):
                if frame_tile(s) <= tile < frame_tile(s) + 6:
                    part = frame_part(s, tile - frame_tile(s), zz)
                    v = part if v is None else v + part
            h[dst, tile * 128 : tile * 128 + 128] = v
        return carry

    around = [send(st1.at[0], st1.at[k + 1], at(dy=d[0], dx=d[1])) for k, d in enumerate(plane)]
    lax.fori_loop(0, NZ // 2, assemble, 0)
    arrive(around)
    total, hit = combine(st1)
    st2[0, 0:4, :] = total
    st2[0, 4:8, :] = hit
    around = [send(st2.at[0], st2.at[k + 1], at(dz=d[0], dc=d[1])) for k, d in enumerate(column)]
    lax.fori_loop(NZ // 2, NZ, assemble, 0)
    arrive(around)
    log_norm, hit = combine(st2)
    norm_row = jnp.concatenate([log_norm[i : i + 1] for i in range(4)], axis=1)

    for b in range(4):
        r = slice(b * 128, b * 128 + 128)
        hot = first_id + b * 128 + lax.broadcasted_iota(jnp.int32, (128, 512), 0) == tgt[...]
        g = tw[...] * (jnp.exp(lt[r, :] - norm_row) - hot.astype(F32))
        pt[r, :] = g.astype(BF16)
        p[:, r] = jnp.transpose(g).astype(BF16)

    def share(s):
        cols = pl.ds(pl.multiple_of(frame_tile(s) * 128, 128), FRAME)
        return lax.dot_general(
            p[...], w[:, cols], (((1,), (0,)), ((), ())), preferred_element_type=F32
        )

    core = []
    for i, o in enumerate(REL):
        gs[i] = share(xo(o) * 2 + other).astype(BF16)
        core.append(send(gs.at[i], rc.at[i], sibling))

    def add_core(i):
        mine[...] = share(xo(REL[i]) * 2 + c)
        core[i].wait_recv()
        for zz in range(NZ):
            r = slice(zz * 64, zz * 64 + 64)
            v = (mine[r, :] + rc[i, r, :].astype(F32)).astype(BF16)
            s0[i, zz] = v[:, 0:256].reshape(NY, 16, LANES)
            for yy in range(NY):
                s1[yy, i, zz] = v[yy * 16 : yy * 16 + 16, 256:512]
            s2[zz, i] = v[:, 512:768].reshape(NY, 16, LANES)

    up, down = pl.ds(0, 4), pl.ds(4, 4)
    up_slice, down_slice = slice(0, 4), slice(4, 8)
    ring0 = {}

    def scatter0():
        yield 6.0
        ring0["ua"].wait_recv()
        s0[1, up_slice] = (s0[1, up_slice].astype(F32) + u0a[...].astype(F32)).astype(BF16)
        ring0["ra"] = send(s0.at[1, up], l0.at[up], x_right)
        ring0["ub"].wait_recv()
        s0[2, down_slice] = (s0[2, down_slice].astype(F32) + u0b[...].astype(F32)).astype(BF16)
        ring0["lb"] = send(s0.at[2, down], m0.at[down], x_left)
        yield 13.0
        arrive([ring0["ra"], ring0["rb"], ring0["la"], ring0["lb"]])
        for zz in range(NZ):
            v = s0[3, zz].astype(F32) + l0[zz].astype(F32) + m0[zz].astype(F32)
            v = v.astype(BF16)
            for yy in range(NY):
                t0[yy, zz] = v[yy]
        e = [send(t0.at[yo(o)], q0.at[o - 1], at(dy=o)) for o in range(1, NY)]
        yield 18.0
        arrive(e)
        c0[...] = sum([q0[k].astype(F32) for k in range(NY - 1)], t0[y].astype(F32))
        e = [send(c0.at[zo(o)], d0.at[o - 1], at(dz=o)) for o in range(1, NZ)]
        yield 23.0
        arrive(e)
        pad[:, 0:256] = sum([d0[k] for k in range(NZ - 1)], c0[z])

    ring1 = {}

    def scatter1():
        yield 7.5
        ring1["ua"].wait_recv()
        r = yo(1)
        s1[r, 0:2] = (s1[r, 0:2].astype(F32) + u1a[...].astype(F32)).astype(BF16)
        ring1["ra"] = send(s1.at[r, pl.ds(0, 2)], l1.at[pl.ds(0, 2)], y_right)
        ring1["ub"].wait_recv()
        r = yo(-1)
        s1[r, 2:4] = (s1[r, 2:4].astype(F32) + u1b[...].astype(F32)).astype(BF16)
        ring1["lb"] = send(s1.at[r, pl.ds(2, 2)], m1.at[pl.ds(2, 2)], y_left)
        yield 13.1
        arrive([ring1["ra"], ring1["rb"], ring1["la"], ring1["lb"]])
        for i in range(NX):
            v = s1[y, i].astype(F32) + l1[i].astype(F32) + m1[i].astype(F32)
            t1[i] = v.astype(BF16)
        e = [send(t1.at[REL.index(o)], q1.at[o - 1], at(dx=o)) for o in range(1, NX)]
        yield 18.1
        arrive(e)
        c1[...] = sum([q1[k].astype(F32) for k in range(NX - 1)], t1[3].astype(F32))
        e = [send(c1.at[zo(o)], d1.at[o - 1], at(dz=o)) for o in range(1, NZ)]
        yield 23.1
        arrive(e)
        pad[:, 256:512] = sum([d1[k] for k in range(NZ - 1)], c1[z])

    right, left = {}, {}

    def scatter2():
        for k in range(1, 4):
            for i in range(NX):
                yield 3.0 + 2.75 * k + 0.7 * i
                if k > 1 or i < 2:
                    right[k, i].wait_recv()
                    r = zo(4 - k)
                    s2[r, i] = (s2[r, i].astype(F32) + l2[k - 1, i].astype(F32)).astype(BF16)
                    right[k + 1, i] = send(s2.at[r, i], l2.at[k, i], z_right)
                if k > 1 or i >= 2:
                    left[k, i].wait_recv()
                    r = zo(k - 4)
                    s2[r, i] = (s2[r, i].astype(F32) + m2[k - 1, i].astype(F32)).astype(BF16)
                    left[k + 1, i] = send(s2.at[r, i], m2.at[k, i], z_left)
        for i in range(NX):
            yield 3.0 + 2.75 * 4 + 0.7 * i
            right[4, i].wait_recv()
            left[4, i].wait_recv()
            v = s2[z, i].astype(F32) + l2[3, i].astype(F32) + m2[3, i].astype(F32)
            t2[i] = v.astype(BF16)
        e = [send(t2.at[REL.index(o)], q2.at[o - 1], at(dx=o)) for o in range(1, NX)]
        yield 20.0
        arrive(e)
        c2[...] = sum([q2[k].astype(F32) for k in range(NX - 1)], t2[3].astype(F32))
        e = [send(c2.at[yo(o)], d2.at[o - 1], at(dy=o)) for o in range(1, NY)]
        yield 23.2
        arrive(e)
        pad[:, 512:768] = sum([d2[k] for k in range(NY - 1)], c2[y])

    for i in range(NX):
        add_core(i)
        if i == 0:
            ring0["ua"] = send(s0.at[0, up], u0a, x_right)
            ring0["ub"] = send(s0.at[0, down], u0b, x_left)
        if i == 1:
            ring0["rb"] = send(s0.at[1, down], l0.at[down], x_right)
        if i == 2:
            ring0["la"] = send(s0.at[2, up], m0.at[up], x_left)
        if i < 2:
            right[1, i] = send(s2.at[zo(4), i], l2.at[0, i], z_right)
            left[2, i] = send(s2.at[zo(-3), i], m2.at[1, i], z_left)
        else:
            left[1, i] = send(s2.at[zo(4), i], m2.at[0, i], z_left)
            right[2, i] = send(s2.at[zo(3), i], l2.at[1, i], z_right)
        if i == 1:
            ring1["ua"] = send(s1.at[yo(2), pl.ds(0, 2)], u1a, y_right)
            ring1["la"] = send(s1.at[yo(-1), pl.ds(0, 2)], m1.at[pl.ds(0, 2)], y_left)
        if i == 3:
            ring1["ub"] = send(s1.at[yo(2), pl.ds(2, 2)], u1b, y_left)
            ring1["rb"] = send(s1.at[yo(1), pl.ds(2, 2)], l1.at[pl.ds(2, 2)], y_right)

    def loss_order():
        yield 12.0
        rows[...] = jnp.zeros_like(rows)
        for i, v in enumerate(pieces(log_norm - hit)):
            rows[i, 0:4, :] = v
        yield 12.5
        src = lax.broadcasted_iota(jnp.int32, (128, 128), 0)
        dst = lax.broadcasted_iota(jnp.int32, (128, 128), 1)
        pick = lax.broadcasted_iota(jnp.int32, (8, 128), 0) == (
            lax.broadcasted_iota(jnp.int32, (8, 128), 1) // 32
        )
        for m in range(4):
            hot = (src == ((dst // 4) % 8) * 16 + m * 4 + dst % 4).astype(BF16)
            v = sum(
                jnp.dot(rows[i].astype(BF16), hot, preferred_element_type=F32)
                for i in range(3)
            )
            loss_ref[m : m + 1, :] = jnp.sum(jnp.where(pick, v, 0.0), axis=0, keepdims=True)

    run_by_time((5.0, scatter2()), (5.0, scatter0()), (5.0, scatter1()), (5.0, loss_order()))

    pad[...] = pltpu.roll(pad[...], lax.rem(FRAME - shift, FRAME), axis=1)
    for m in range(4):
        gh_ref[m] = pad[4 * m : 4 * m + 4, 0:672].astype(BF16)

    for copy in sends:
        copy.wait_send()


def weight_kernel(pt_ref, h_ref, gw_ref):
    cols = pl.ds(pl.multiple_of(pl.program_id(0) * FRAME, 128), FRAME)
    gw_ref[...] = lax.dot_general(
        pt_ref[...], h_ref[:, cols], (((1,), (0,)), ((), ())), preferred_element_type=F32
    ).astype(BF16)


def per_device(final_hidden, out_weight, targets, token_weight):
    vm, dma = pltpu.VMEM, pltpu.SemaphoreType.DMA
    scratch = [
        vm((512, 5376), BF16),
        vm((512, 512), F32),
        vm((512, 512), BF16),
        vm((16, FRAME), F32),
        vm((512, FRAME), F32),
        vm((4, 8, 128), F32),
        vm((1, 512), jnp.int32),
        vm((1, 512), F32),
        vm((2, NX, NZ, NY, 16, LANES), BF16),
        vm((2, NX, NZ, NY, 16, LANES), BF16),
        vm((2, NX, NZ, NY, 16, LANES), BF16),
        vm((NX, 512, FRAME), BF16),
        vm((NX, 512, FRAME), BF16),
        vm((NX, NZ, NY, 16, LANES), BF16),
        vm((NY, NX, NZ, 16, LANES), BF16),
        vm((NZ, NX, NY, 16, LANES), BF16),
        vm((4, NY, 16, LANES), BF16),
        vm((4, NY, 16, LANES), BF16),
        vm((NZ, NY, 16, LANES), BF16),
        vm((NZ, NY, 16, LANES), BF16),
        vm((2, NZ, 16, LANES), BF16),
        vm((2, NZ, 16, LANES), BF16),
        vm((NX, NZ, 16, LANES), BF16),
        vm((NX, NZ, 16, LANES), BF16),
        vm((4, NX, NY, 16, LANES), BF16),
        vm((4, NX, NY, 16, LANES), BF16),
        vm((NY, NZ, 16, LANES), BF16),
        vm((NX, NZ, 16, LANES), BF16),
        vm((NX, NY, 16, LANES), BF16),
        vm((NY - 1, NZ, 16, LANES), BF16),
        vm((NX - 1, NZ, 16, LANES), BF16),
        vm((NX - 1, NY, 16, LANES), BF16),
        vm((NZ, 16, LANES), F32),
        vm((NZ, 16, LANES), F32),
        vm((NY, 16, LANES), F32),
        vm((NZ - 1, 16, LANES), F32),
        vm((NZ - 1, 16, LANES), F32),
        vm((NY - 1, 16, LANES), F32),
        vm((16, 8, 128), F32),
        vm((16, 8, 128), F32),
        dma, dma((COPIES,)), dma((COPIES,)),
    ]
    vmem = pl.BlockSpec(memory_space=pltpu.VMEM)
    hbm = pl.BlockSpec(memory_space=pl.ANY)
    loss, grad_hidden, hidden, grads = pl.pallas_call(
        kernel,
        out_shape=(
            jax.ShapeDtypeStruct((4, 128), F32),
            jax.ShapeDtypeStruct((4, 4, 672), BF16),
            pltpu.VMEM((512, 5376), BF16),
            pltpu.VMEM((512, 512), BF16),
        ),
        in_specs=[vmem, hbm, vmem, vmem],
        out_specs=(vmem, vmem, vmem, vmem),
        scratch_shapes=scratch,
        compiler_params=pltpu.CompilerParams(
            collective_id=0, has_side_effects=True, vmem_limit_bytes=48 * 2**20
        ),
        name="xent",
    )(final_hidden, out_weight, targets, token_weight)
    grads = pltpu.with_memory_space_constraint(grads, pltpu.VMEM)
    hidden = pltpu.with_memory_space_constraint(hidden, pltpu.VMEM)
    grad_weight = pl.pallas_call(
        weight_kernel,
        grid=(7,),
        out_shape=jax.ShapeDtypeStruct((512, 5376), BF16),
        in_specs=[vmem, vmem],
        out_specs=pl.BlockSpec((512, FRAME), lambda k: (0, k)),
        compiler_params=pltpu.CompilerParams(vmem_limit_bytes=12 * 2**20),
        name="weight_grad",
    )(grads, hidden)
    return (loss, grad_hidden, grad_weight)


def solution(mesh):
    in_specs = (P(None, "dp", "section"), P(("dp", "section"), None), P(), P())
    out_specs = (P(), P(None, "dp", "section"), P(("dp", "section"), None))
    return jax.shard_map(
        per_device, mesh=mesh, in_specs=in_specs, out_specs=out_specs, check_vma=False
    )
```

time: 606 us -> 91.1 us (0.15)
  waiting for transfers between devices: 356 us -> 0 us
  blocking collectives: 176 us -> 0 us
  Pallas kernels: 0 us -> 86.7 us
  local copies, waits for them, and re-layouts: 34.2 us -> 3.28 us
  matrix products: 23 us -> 0 us
  between operations: 14.5 us -> 0.65 us
    unnamed x5 -> x0, waiting for transfers between devices: 269 us -> none
    all_gather x1 -> x0, waiting for transfers between devices: 86.9 us -> none  [per_device(): gathered = lax.all_gather(features, 'dp', axis=1, tiled=True)]
    pallas_call x0 -> x2, Pallas kernels: none -> 86.7 us  [the longest x1 80.8 us: per_device(): pl.pallas_call(kernel, out_shape=(jax.ShapeDtypeStruct((4, 128), F32), ja...]
    psum x1 -> x0, blocking collectives: 73.9 us -> none  [per_device(): summed, picked = lax.psum((local_total, picked_local), ('dp', 'section'))]
    pmax x1 -> x0, blocking collectives: 73.7 us -> none  [per_device(): highest = lax.pmax(local_top, ('dp', 'section'))]
    all_gather x1 -> x0, blocking collectives: 28.4 us -> none  [per_device(): features = lax.all_gather(final_hidden, 'section', axis=2, tiled=True)]
    dot_general x3 -> x0, matrix products: 23 us -> none  [the longest x1 8.38 us: per_device(): jnp.dot(logit_grads, out_weight, preferred_element_type=jnp.float32)]
    unnamed x15 -> x8, local copies, waits for them, and re-layouts: 22.8 us -> 3.28 us
  transfers between devices with their start and end apart: 3 -> 0, of which waited for: 3 -> 0; matrix products, arithmetic and copies ran while one was open for 1% -> 0% of each run, Pallas kernels for 0% -> 0%
where the time goes in v2:
time: 91.1 us; the launch traced here: 90.6 us
  Pallas kernels  86.7 us (95%)
  local copies, waits for them, and re-layouts  3.28 us (4%)
    pallas_call x1, Pallas kernels, per_device(): pl.pallas_call(kernel, out_shape=(jax.ShapeDtypeStruct((4, 128), F32), ja...  80.8 us
    pallas_call x1, Pallas kernels, per_device(): pl.pallas_call(weight_kernel, grid=(7,), out_shape=jax.ShapeDtypeStruct((...  5.85 us
    unnamed x8, local copies, waits for them, and re-layouts  3.28 us

profile of v2, /device:TPU:8, one launch (start us, length us, event | category | flops | bytes accessed | tf_op | source)
XLA Modules:
  0.0 90.6 jit_solution(5269149448009912992)
XLA Ops:
  0.6 0.0 copy-start
  0.6 0.7 copy-done
  1.4 0.0 copy-start.1
  1.4 0.7 copy-done.1
  2.1 0.0 copy-start.2
  2.1 0.7 copy-done.2
  2.7 80.8 %xent.1 = (f32[4,128]{1,0:T(4,128)S(1)}, bf16[4,4,672]{2,1,0:T(4,128)(2,1)S(1)}, bf16[512,5376]{1,0:T(8,128)(2,1)S(1)}, bf16[512,512]{1,0:T(8,128)(2,1)S(1)}) custom-call(bf16[4,4,672]{2,1,0:T(4,128)(2,1)S(1)} %copy-done, bf16[512,5376]{1,0:T(8,128)(2,1)} %w_hbm.1, s32[4,128]{1,0:T(4,128)S(1)} %copy-done.1, f32[4,128]{1,0:T(4,128)S(1)} %copy-done.2), custom_call_target="tpu_custom_call" | custom-call | tf_op jit(solution)/shard_map/xent/pallas_call | solution.py:522
  83.6 5.8 %weight_grad.1 = bf16[512,5376]{1,0:T(8,128)(2,1)} custom-call(bf16[512,512]{1,0:T(8,128)(2,1)S(1)} %get-tuple-element.9.pt_ref, bf16[512,5376]{1,0:T(8,128)(2,1)S(1)} %get-tuple-element.10.h_ref), custom_call_target="tpu_custom_call" | custom-call | tf_op jit(solution)/shard_map/weight_grad/pallas_call | solution.py:540
  89.4 0.6 copy.9
  90.0 0.6 copy.10
Async XLA Ops:
  0.6 0.7 copy-start
  1.4 0.7 copy-start.1
  2.1 0.7 copy-start.2

commit v3 on v0

v3 whole, which is shorter than its diff:
```python
import heapq
import math

import jax
import jax.numpy as jnp
from jax import lax
from jax.experimental import pallas as pl
from jax.experimental.pallas import tpu as pltpu
from jax.sharding import PartitionSpec as P

MESH = pl.DeviceIdType.MESH
F32, BF16 = jnp.float32, jnp.bfloat16
NX, NY, NZ = 4, 4, 8
FRAME = 768
PARTS = 3
LANES = 128
HALVES = 2
TOKENS = 256
REL = (2, 1, 3, 0)
SENDS, GROUPS = 7, 110


def frame_tile(section):
    return (21 * section) // 4


def run_by_time(tasks):
    heap = []
    for k, (start, task) in enumerate(tasks):
        heapq.heappush(heap, (start, k, task))
    while heap:
        _, k, task = heapq.heappop(heap)
        try:
            heapq.heappush(heap, (next(task), k, task))
        except StopIteration:
            pass


def pieces(v):
    hi = v.astype(BF16).astype(F32)
    mid = (v - hi).astype(BF16).astype(F32)
    return hi, mid, v - hi - mid


def kernel(
    h_hbm, w_hbm, tgt_hbm, tw_hbm,
    loss_ref, gh_ref, gw,
    h_ref, tgt_ref, tw_ref, h, pt, w, lt, p, pad, mine, rows, tgt, tw,
    a01, a2,
    gs, rc, s0, s1, s2, u0a, u0b, l0, m0, u1a, u1b, l1, m1, l2, m2,
    t0, t1, t2, q0, q1, q2, c01, c2, d01, d2,
    st1, st2,
    in_sem, send_sem, recv_sem,
):
    dp = lax.axis_index("dp")
    section = lax.axis_index("section")
    z, y = dp // NY, dp % NY
    x, c = section // 2, section % 2
    other = 1 - c

    def at(dz=0, dy=0, dx=0, dc=0):
        return (
            lax.rem(z + dz, NZ) * NY + lax.rem(y + dy, NY),
            lax.rem(x + dx, NX) * 2 + lax.rem(c + dc, 2),
        )

    def zo(o):
        return lax.rem(z + o + NZ, NZ)

    def yo(o):
        return lax.rem(y + o + NY, NY)

    def xo(o):
        return lax.rem(x + o + NX, NX)

    sibling = at(dc=1)
    x_right, x_left = at(dx=1), at(dx=3)
    y_right, y_left = at(dy=1), at(dy=3)
    z_right, z_left = at(dz=1), at(dz=7)

    load_h = pltpu.make_async_copy(h_hbm, h_ref, in_sem.at[0])
    load_tgt = pltpu.make_async_copy(tgt_hbm, tgt_ref, in_sem.at[1])
    load_tw = pltpu.make_async_copy(tw_hbm, tw_ref, in_sem.at[2])
    load_w = pltpu.make_async_copy(w_hbm, w, in_sem.at[3])
    for load in (load_h, load_tgt, load_tw):
        load.start()

    plane = [(k // NX, k % NX) for k in range(1, NX * NY)]
    column = [(k // 2, k % 2) for k in range(1, NZ * 2)]
    barrier = pltpu.get_barrier_semaphore()
    for dy, dx in plane:
        pl.semaphore_signal(barrier, inc=1, device_id=at(dy=dy, dx=dx), device_id_type=MESH)
    for dz, dc in column:
        pl.semaphore_signal(barrier, inc=1, device_id=at(dz=dz, dc=dc), device_id_type=MESH)

    rows[...] = jnp.zeros_like(rows)
    pad[...] = jnp.zeros_like(pad)
    st1[...] = jnp.zeros_like(st1)
    st2[...] = jnp.zeros_like(st2)
    load_h.wait()
    for m in range(4):
        pad[4 * m : 4 * m + 4, 0:672] = h_ref[m].astype(F32)
    shift = lax.rem(section, 4) * 32
    framed = pltpu.roll(pad[...], shift, axis=1)
    for q in range(HALVES):
        v = framed[8 * q : 8 * q + 8]
        packed = [
            jnp.concatenate([v[:, j : j + 128], v[:, j + 128 : j + 256]], axis=0).astype(BF16)
            for j in (0, 256, 512)
        ]
        a01[q, c, x, z, y, :, 0:128] = packed[0]
        a01[q, c, x, z, y, :, 128:256] = packed[1]
        a2[q, c, x, z, y] = packed[2]

    pl.semaphore_wait(barrier, len(plane) + len(column))

    def wait_tiles(sem, tiles, sent):
        r = max(d for d in range(1, 33) if tiles % d == 0 and tiles // d <= 42)
        ref = h.at[pl.ds(0, 16 * r), pl.ds(0, 128 * (tiles // r))]
        copy = pltpu.make_async_remote_copy(
            src_ref=ref, dst_ref=ref, send_sem=sem, recv_sem=sem,
            device_id=sibling, device_id_type=MESH,
        )
        if sent:
            copy.wait_send()
        else:
            copy.wait_recv()

    groups = []
    sends = [0]

    def group():
        groups.append(0)
        return len(groups) - 1

    def send(src, dst, device, g):
        tiles = math.prod(src.shape) * jnp.dtype(src.dtype).itemsize // 4096
        if sends[-1] >= 500 and any(
            sends[-1] % d == 0 and sends[-1] // d <= 42 for d in range(1, 33)
        ):
            sends.append(0)
        groups[g] += tiles
        sends[-1] += tiles
        pltpu.make_async_remote_copy(
            src_ref=src, dst_ref=dst, send_sem=send_sem.at[len(sends) - 1],
            recv_sem=recv_sem.at[g], device_id=device, device_id_type=MESH,
        ).start()

    def arrive(g):
        wait_tiles(recv_sem.at[g], groups[g], False)

    def gather(ref, axis, n):
        g = group()
        for o in range(1, n):
            send(ref, ref, at(**{"d" + axis: o}), g)
        return g

    done = set()

    def finish(name):
        done.add(name)

    from_sibling01 = [group() for _ in range(HALVES)]
    from_sibling2 = [group() for _ in range(HALVES)]

    def gather01(q, t):
        first, second = pl.ds(0, 128), pl.ds(128, 128)

        def pass_on(ref):
            send(ref, ref, sibling, from_sibling01[q])

        def part0(o, half):
            return a01.at[q, c, xo(o), pl.ds(4 * half, 4), :, :, first]

        def part1(o, half):
            return a01.at[q, c, pl.ds(2 * half, 2), :, yo(o), :, second]

        e = gather(a01.at[q, c, x, z, y], "z", NZ)
        yield t[0]
        arrive(e)
        e0 = gather(a01.at[q, c, x, :, y, :, first], "y", NY)
        e1 = gather(a01.at[q, c, x, :, y, :, second], "x", NX)
        yield t[1]
        rings = []
        for e, part, right, left in (
            (e0, part0, x_right, x_left), (e1, part1, y_right, y_left)
        ):
            arrive(e)
            near, far = group(), group()
            rings.append((part, right, left, near, far))
            send(part(0, 0), part(0, 0), right, near)
            send(part(0, 1), part(0, 1), left, near)
            send(part(0, 1), part(0, 1), right, far)
            send(part(0, 0), part(0, 0), left, far)
        pass_on(a01.at[q, c, x, :, :, :, first])
        pass_on(a01.at[q, c, :, :, y, :, second])
        yield t[2]
        last = []
        for part, right, left, near, far in rings:
            arrive(near)
            g = group()
            last.append(g)
            send(part(-1, 0), part(-1, 0), right, g)
            send(part(1, 1), part(1, 1), left, g)
        yield t[3]
        arrive(rings[0][4])
        pass_on(a01.at[q, c, xo(-1), :, :, :, first])
        pass_on(a01.at[q, c, xo(1), :, :, :, first])
        arrive(rings[1][4])
        pass_on(a01.at[q, c, :, :, yo(-1), :, second])
        pass_on(a01.at[q, c, :, :, yo(1), :, second])
        yield t[4]
        arrive(last[0])
        pass_on(a01.at[q, c, xo(2), :, :, :, first])
        arrive(last[1])
        pass_on(a01.at[q, c, :, :, yo(2), :, second])
        finish(("gather01", q))

    def gather2(q, t):
        def pass_on(ref):
            send(ref, ref, sibling, from_sibling2[q])

        def part(o, i):
            return a2.at[q, c, i, zo(o)]

        e = gather(a2.at[q, c, x, z, y], "x", NX)
        yield t[0]
        arrive(e)
        e = gather(a2.at[q, c, :, z, y], "y", NY)
        yield t[1]
        arrive(e)
        hop = [group() for _ in range(NX)]
        for i in range(NX):
            k = NX - 1 - i
            send(part(0, i), part(0, i), z_right, hop[i])
            send(part(0, k), part(0, k), z_left, hop[i])
        pass_on(a2.at[q, c, :, z])
        for o in (1, 2, 3):
            after = [group() for _ in range(NX)] if o < 3 else [group()] * 2
            for i in range(NX):
                yield t[1] + o * t[2] + i * 0.3
                arrive(hop[i])
                k = NX - 1 - i
                if o < 3 or i < 2:
                    send(part(-o, i), part(-o, i), z_right, after[i])
                    send(part(o, k), part(o, k), z_left, after[i])
            hop = after
            pass_on(a2.at[q, c, :, zo(-o)])
            pass_on(a2.at[q, c, :, zo(o)])
        yield t[1] + 4 * t[2] + 0.3
        arrive(hop[0])
        pass_on(a2.at[q, c, :, zo(4)])
        finish(("gather2", q))

    def token_order():
        load_w.start()
        yield 1.0
        load_tgt.wait()
        load_tw.wait()
        t = tgt_ref[...]
        parts = [(t & 63).astype(F32), ((t >> 6) & 63).astype(F32), (t >> 12).astype(F32)]
        parts += list(pieces(tw_ref[...]))
        for i in range(6):
            for m in range(4):
                rows[m, i : i + 1, :] = parts[i][m : m + 1, :]
        src = lax.broadcasted_iota(jnp.int32, (128, 512), 0)
        dst = lax.broadcasted_iota(jnp.int32, (128, 512), 1)
        out = jnp.zeros((8, 512), F32)
        for m in range(4):
            hot = dst == (m // 2) * TOKENS + (src // 4) * 8 + (m % 2) * 4 + src % 4
            out += jnp.dot(
                rows[m].astype(BF16), hot.astype(BF16), preferred_element_type=F32
            )
        number = out[0:1].astype(jnp.int32) + out[1:2].astype(jnp.int32) * 64
        tgt[...] = number + out[2:3].astype(jnp.int32) * 4096
        tw[...] = out[3:4] + out[4:5] + out[5:6]

    first_id = (dp * (NX * 2) + section) * 512

    def combine(buf):
        v = buf[...]
        m = jnp.max(v[:, 0:2], axis=0)
        total = m + jnp.log(jnp.sum(jnp.exp(v[:, 0:2] - m[None]), axis=0))
        return total, jnp.sum(v[:, 2:4], axis=0)

    def frame_part(q, s, tile, zz):
        j, low = tile // 2, (tile % 2) * 8
        if j == 2:
            v = a2[q, s % 2, s // 2, zz]
        else:
            v = a01[q, s % 2, s // 2, zz, :, :, j * 128 : j * 128 + 128]
        return v.astype(F32)[:, low : low + 8].reshape(NY * 8, 128)

    def assemble(q, first, last):
        def step(zz, carry):
            dst = pl.ds(pl.multiple_of(q * TOKENS + zz * 32, 32), 32)
            for tile in range(42):
                v = None
                for s in range(8):
                    if frame_tile(s) <= tile < frame_tile(s) + 6:
                        part = frame_part(q, s, tile - frame_tile(s), zz)
                        v = part if v is None else v + part
                h[dst, tile * 128 : tile * 128 + 128] = v.astype(BF16)
            return carry

        lax.fori_loop(first, last, step, 0)

    def loss_order(q, loss):
        for i, v in enumerate(pieces(loss)):
            rows[i] = jnp.concatenate([v, jnp.zeros((6, 128), F32)], axis=0)
        src = lax.broadcasted_iota(jnp.int32, (128, 128), 0)
        dst = lax.broadcasted_iota(jnp.int32, (128, 128), 1)
        pick = lax.broadcasted_iota(jnp.int32, (8, 128), 0) == (
            lax.broadcasted_iota(jnp.int32, (8, 128), 1) // 64
        )
        for m in (0, 1):
            hot = (src == ((dst // 4) % 16) * 8 + m * 4 + dst % 4).astype(BF16)
            v = sum(
                jnp.dot(rows[i].astype(BF16), hot, preferred_element_type=F32)
                for i in range(3)
            )
            k = 2 * q + m
            loss_ref[k : k + 1, :] = jnp.sum(jnp.where(pick, v, 0.0), axis=0, keepdims=True)

    def share(q, s):
        cols = pl.ds(pl.multiple_of(frame_tile(s) * 128, 128), FRAME)
        return lax.dot_general(
            p[q], w[:, cols], (((1,), (0,)), ((), ())), preferred_element_type=F32
        )

    up, down = pl.ds(0, 4), pl.ds(4, 4)
    up_slice, down_slice = slice(0, 4), slice(4, 8)
    front, back = pl.ds(0, 2), pl.ds(2, 2)
    near0, near1, far0, far1 = ([group() for _ in range(HALVES)] for _ in range(4))
    ring2 = [
        {(k, i): group() for k in (1, 2, 3, 4) for i in range(NX) if k > 1 or i < 2}
        for _ in range(HALVES)
    ]
    tasks = []

    def main(q, t):
        cols = slice(q * TOKENS, q * TOKENS + TOKENS)
        yield t[0]
        assert ("gather01", q) in done and ("gather2", q) in done
        arrive(from_sibling01[q])
        arrive(from_sibling2[q])
        if q == 0:
            load_w.wait()
        for k in range(4):
            assemble(q, 2 * k, 2 * k + 2)
            yield t[0] + 0.4 * (k + 1)
        for k in range(7):
            feats = slice(k * 768, k * 768 + 768)
            v = lax.dot_general(
                w[:, feats], h[cols, feats], (((1,), (1,)), ((), ())),
                preferred_element_type=F32,
            )
            if k == 0:
                lt[q] = v
            else:
                lt[q] += v
            yield t[0] + 1.6 + 0.2 * (k + 1)
        ids = first_id + lax.broadcasted_iota(jnp.int32, (512, TOKENS), 0)
        logits = lt[q]
        picked = jnp.sum(jnp.where(ids == tgt[:, cols], logits, 0.0), axis=0, keepdims=True)
        top = jnp.max(logits, axis=0, keepdims=True)
        lse = top + jnp.log(jnp.sum(jnp.exp(logits - top), axis=0, keepdims=True))
        for i in range(2):
            st1[q, 0, i : i + 1, :] = lse[:, i * 128 : i * 128 + 128]
            st1[q, 0, 2 + i : 3 + i, :] = picked[:, i * 128 : i * 128 + 128]
        around = group()
        for k, d in enumerate(plane):
            send(st1.at[q, 0], st1.at[q, k + 1], at(dy=d[0], dx=d[1]), around)
        yield t[1]
        arrive(around)
        total, hit = combine(st1.at[q])
        st2[q, 0, 0:2, :] = total
        st2[q, 0, 2:4, :] = hit
        around = group()
        for k, d in enumerate(column):
            send(st2.at[q, 0], st2.at[q, k + 1], at(dz=d[0], dc=d[1]), around)
        yield t[2]
        arrive(around)
        log_norm, hit = combine(st2.at[q])
        norm_row = jnp.concatenate([log_norm[i : i + 1] for i in range(2)], axis=1)
        for b in range(4):
            r = slice(b * 128, b * 128 + 128)
            ids = first_id + b * 128 + lax.broadcasted_iota(jnp.int32, (128, TOKENS), 0)
            hot = (ids == tgt[:, cols]).astype(F32)
            g = tw[:, cols] * (jnp.exp(lt[q, r, :] - norm_row) - hot)
            pt[r, cols] = g.astype(BF16)
            p[q, :, r] = jnp.transpose(g).astype(BF16)
        core = []
        for i, o in enumerate(REL):
            gs[q, i] = share(q, xo(o) * 2 + other).astype(BF16)
            core.append(group())
            send(gs.at[q, i], rc.at[q, i], sibling, core[i])
        for i in range(NX):
            yield t[3] + i * 0.7
            mine[...] = share(q, xo(REL[i]) * 2 + c)
            arrive(core[i])
            for zz in range(NZ):
                r = slice(zz * 32, zz * 32 + 32)
                v = mine[r, :] + rc[q, i, r, :].astype(F32)
                for yy in range(NY):
                    u = v[yy * 8 : yy * 8 + 8]
                    packed = [
                        jnp.concatenate(
                            [u[:, j : j + 128], u[:, j + 128 : j + 256]], axis=0
                        ).astype(BF16)
                        for j in (0, 256, 512)
                    ]
                    s0[q, i, zz, yy] = packed[0]
                    s1[q, yy, i, zz] = packed[1]
                    s2[q, zz, i, yy] = packed[2]
            first_sends(q, i)
        loss_order(q, log_norm - hit)
        finish(("main", q))

    def first_sends(q, i):
        if i == 0:
            send(s0.at[q, 0, up], u0a.at[q], x_right, near0[q])
            send(s0.at[q, 0, down], u0b.at[q], x_left, near0[q])
        k = NX - 1 - i
        if i < 2:
            send(s2.at[q, zo(4), i], l2.at[q, 0, i], z_right, ring2[q][1, i])
            send(s2.at[q, zo(-3), i], m2.at[q, 1, i], z_left, ring2[q][2, k])
        else:
            send(s2.at[q, zo(4), i], m2.at[q, 0, i], z_left, ring2[q][1, k])
            send(s2.at[q, zo(3), i], l2.at[q, 1, i], z_right, ring2[q][2, i])
        if i == 1:
            send(s1.at[q, yo(2), front], u1a.at[q], y_right, near1[q])
            send(s1.at[q, yo(-1), front], m1.at[q, front], y_left, far1[q])
            send(s0.at[q, 1, down], l0.at[q, down], x_right, far0[q])
        if i == 2:
            send(s0.at[q, 2, up], m0.at[q, up], x_left, far0[q])
        if i == 3:
            send(s1.at[q, yo(2), back], u1b.at[q], y_left, near1[q])
            send(s1.at[q, yo(1), back], l1.at[q, back], y_right, far1[q])

    def scatter01(q, t):
        yield t[0]
        arrive(near0[q])
        s0[q, 1, up_slice] = (
            s0[q, 1, up_slice].astype(F32) + u0a[q].astype(F32)
        ).astype(BF16)
        send(s0.at[q, 1, up], l0.at[q, up], x_right, far0[q])
        s0[q, 2, down_slice] = (
            s0[q, 2, down_slice].astype(F32) + u0b[q].astype(F32)
        ).astype(BF16)
        send(s0.at[q, 2, down], m0.at[q, down], x_left, far0[q])
        yield t[1]
        assert ("main", q) in done
        arrive(near1[q])
        r = yo(1)
        s1[q, r, 0:2] = (s1[q, r, 0:2].astype(F32) + u1a[q].astype(F32)).astype(BF16)
        send(s1.at[q, r, front], l1.at[q, front], y_right, far1[q])
        r = yo(-1)
        s1[q, r, 2:4] = (s1[q, r, 2:4].astype(F32) + u1b[q].astype(F32)).astype(BF16)
        send(s1.at[q, r, back], m1.at[q, back], y_left, far1[q])
        yield t[2]
        arrive(far0[q])
        for zz in range(NZ):
            v = s0[q, 3, zz].astype(F32) + l0[q, zz].astype(F32) + m0[q, zz].astype(F32)
            v = v.astype(BF16)
            for yy in range(NY):
                t0[q, yy, zz] = v[yy]
        e0 = group()
        for o in range(1, NY):
            send(t0.at[q, yo(o)], q0.at[q, o - 1], at(dy=o), e0)
        yield t[2] + 0.1
        arrive(far1[q])
        for i in range(NX):
            v = s1[q, y, i].astype(F32) + l1[q, i].astype(F32) + m1[q, i].astype(F32)
            t1[q, i] = v.astype(BF16)
        e1 = group()
        for o in range(1, NX):
            send(t1.at[q, REL.index(o)], q1.at[q, o - 1], at(dx=o), e1)
        yield t[3]
        arrive(e0)
        c01[q, :, :, 0:128] = sum(
            [q0[q, k].astype(F32) for k in range(NY - 1)], t0[q, y].astype(F32)
        )
        arrive(e1)
        c01[q, :, :, 128:256] = sum(
            [q1[q, k].astype(F32) for k in range(NX - 1)], t1[q, 3].astype(F32)
        )
        e = group()
        for o in range(1, NZ):
            send(c01.at[q, zo(o)], d01.at[q, o - 1], at(dz=o), e)
        yield t[4]
        arrive(e)
        v = sum([d01[q, k] for k in range(NZ - 1)], c01[q, z])
        r = slice(8 * q, 8 * q + 8)
        pad[r, 0:128] = v[0:8, 0:128]
        pad[r, 128:256] = v[8:16, 0:128]
        pad[r, 256:384] = v[0:8, 128:256]
        pad[r, 384:512] = v[8:16, 128:256]
        finish(("scatter01", q))
        write_hidden(q)

    def scatter2(q, t):
        for k in (1, 2, 3):
            for i in range(NX):
                if k == 1 and i > 1:
                    continue
                yield t[0] + (k - 1) * t[1] + i * 0.3
                assert ("main", q) in done or k == 1
                arrive(ring2[q][k, i])
                j = NX - 1 - i
                r = zo(4 - k)
                v = s2[q, r, i].astype(F32) + l2[q, k - 1, i].astype(F32)
                s2[q, r, i] = v.astype(BF16)
                send(s2.at[q, r, i], l2.at[q, k, i], z_right, ring2[q][k + 1, i])
                r = zo(k - 4)
                v = s2[q, r, j].astype(F32) + m2[q, k - 1, j].astype(F32)
                s2[q, r, j] = v.astype(BF16)
                send(s2.at[q, r, j], m2.at[q, k, j], z_left, ring2[q][k + 1, i])
        yield t[0] + 3 * t[1] + 0.9
        for i in range(NX):
            arrive(ring2[q][4, i])
        for i in range(NX):
            v = s2[q, z, i].astype(F32) + l2[q, 3, i].astype(F32) + m2[q, 3, i].astype(F32)
            t2[q, i] = v.astype(BF16)
        e = group()
        for o in range(1, NX):
            send(t2.at[q, REL.index(o)], q2.at[q, o - 1], at(dx=o), e)
        yield t[2]
        arrive(e)
        c2[q] = sum([q2[q, k].astype(F32) for k in range(NX - 1)], t2[q, 3].astype(F32))
        e = group()
        for o in range(1, NY):
            send(c2.at[q, yo(o)], d2.at[q, o - 1], at(dy=o), e)
        yield t[3]
        arrive(e)
        v = sum([d2[q, k] for k in range(NY - 1)], c2[q, y])
        r = slice(8 * q, 8 * q + 8)
        pad[r, 512:640] = v[0:8]
        pad[r, 640:768] = v[8:16]
        finish(("scatter2", q))
        write_hidden(q)

    def write_hidden(q):
        if ("scatter01", q) in done and ("scatter2", q) in done:
            r = slice(8 * q, 8 * q + 8)
            v = pltpu.roll(pad[r, :], lax.rem(FRAME - shift, FRAME), axis=1)
            pad[r, :] = v
            for m in (0, 1):
                k = 8 * q + 4 * m
                gh_ref[2 * q + m] = pad[k : k + 4, 0:672].astype(BF16)

    def weight(t):
        for k in range(14):
            yield t + 0.7 * k
            assert ("main", 0) in done and ("main", 1) in done
            feats = slice(k * 384, k * 384 + 384)
            gw[:, feats] = lax.dot_general(
                pt[...], h[:, feats], (((1,), (0,)), ((), ())), preferred_element_type=F32
            ).astype(BF16)

    run_by_time(
        [
            (0.0, gather01(0, (4.6, 8.2, 10.7, 12.4, 14.2))),
            (0.1, gather2(0, (2.4, 5.2, 2.5))),
            (0.2, gather01(1, (5.4, 9.2, 12.8, 15.0, 17.0))),
            (0.3, gather2(1, (2.6, 5.6, 2.8))),
            (0.9, token_order()),
            (16.6, main(0, (16.6, 24.3, 28.8, 30.5))),
            (19.0, main(1, (19.0, 27.0, 31.5, 34.0))),
            (34.0, scatter01(0, (34.0, 35.0, 38.0, 42.0, 47.0))),
            (34.0, scatter2(0, (35.0, 2.5, 45.0, 47.5))),
            (37.5, scatter01(1, (37.5, 38.7, 42.5, 46.0, 51.0))),
            (38.0, scatter2(1, (38.6, 2.5, 48.5, 51.0))),
            (38.0, weight(38.0)),
        ]
    )

    for k, tiles in enumerate(sends):
        wait_tiles(send_sem.at[k], tiles, True)
    assert len(sends) == SENDS and len(groups) == GROUPS, (len(sends), len(groups))


def store_kernel(loss, gh, gw, loss_out, gh_out, gw_out, sem):
    copies = [
        pltpu.make_async_copy(loss, loss_out, sem.at[8]),
        pltpu.make_async_copy(gh, gh_out, sem.at[9]),
    ]
    for k in range(8):
        r = pl.ds(64 * k, 64)
        copies.append(pltpu.make_async_copy(gw.at[r], gw_out.at[r], sem.at[k]))
    for copy in copies:
        copy.start()
    for copy in copies:
        copy.wait()


def per_device(final_hidden, out_weight, targets, token_weight):
    vm, dma = pltpu.VMEM, pltpu.SemaphoreType.DMA
    n = HALVES
    scratch = [
        vm((4, 4, 672), BF16),
        vm((4, 128), jnp.int32),
        vm((4, 128), F32),
        vm((512, 5376), BF16),
        vm((512, 512), BF16),
        vm((512, 5376), BF16),
        vm((n, 512, TOKENS), F32),
        vm((n, TOKENS, 512), BF16),
        vm((16, FRAME), F32),
        vm((TOKENS, FRAME), F32),
        vm((4, 8, 128), F32),
        vm((1, 512), jnp.int32),
        vm((1, 512), F32),
        vm((n, 2, NX, NZ, NY, 16, 2 * LANES), BF16),
        vm((n, 2, NX, NZ, NY, 16, LANES), BF16),
        vm((n, NX, TOKENS, FRAME), BF16),
        vm((n, NX, TOKENS, FRAME), BF16),
        vm((n, NX, NZ, NY, 16, LANES), BF16),
        vm((n, NY, NX, NZ, 16, LANES), BF16),
        vm((n, NZ, NX, NY, 16, LANES), BF16),
        vm((n, 4, NY, 16, LANES), BF16),
        vm((n, 4, NY, 16, LANES), BF16),
        vm((n, NZ, NY, 16, LANES), BF16),
        vm((n, NZ, NY, 16, LANES), BF16),
        vm((n, 2, NZ, 16, LANES), BF16),
        vm((n, 2, NZ, 16, LANES), BF16),
        vm((n, NX, NZ, 16, LANES), BF16),
        vm((n, NX, NZ, 16, LANES), BF16),
        vm((n, 4, NX, NY, 16, LANES), BF16),
        vm((n, 4, NX, NY, 16, LANES), BF16),
        vm((n, NY, NZ, 16, LANES), BF16),
        vm((n, NX, NZ, 16, LANES), BF16),
        vm((n, NX, NY, 16, LANES), BF16),
        vm((n, NY - 1, NZ, 16, LANES), BF16),
        vm((n, NX - 1, NZ, 16, LANES), BF16),
        vm((n, NX - 1, NY, 16, LANES), BF16),
        vm((n, NZ, 16, 2 * LANES), F32),
        vm((n, NY, 16, LANES), F32),
        vm((n, NZ - 1, 16, 2 * LANES), F32),
        vm((n, NY - 1, 16, LANES), F32),
        vm((n, 16, 8, 128), F32),
        vm((n, 16, 8, 128), F32),
        dma((4,)), dma((SENDS,)), dma((GROUPS,)),
    ]
    vmem = pl.BlockSpec(memory_space=pltpu.VMEM)
    hbm = pl.BlockSpec(memory_space=pl.ANY)
    final_hidden, targets, token_weight = (
        pltpu.with_memory_space_constraint(v, pltpu.HBM)
        for v in (final_hidden, targets, token_weight)
    )
    loss, grad_hidden, grad_weight = pl.pallas_call(
        kernel,
        out_shape=(
            pltpu.VMEM((4, 128), F32),
            pltpu.VMEM((4, 4, 672), BF16),
            pltpu.VMEM((512, 5376), BF16),
        ),
        in_specs=[hbm, hbm, hbm, hbm],
        out_specs=(vmem, vmem, vmem),
        scratch_shapes=scratch,
        compiler_params=pltpu.CompilerParams(
            collective_id=0, has_side_effects=True, vmem_limit_bytes=48 * 2**20
        ),
        name="xent",
    )(final_hidden, out_weight, targets, token_weight)
    return pl.pallas_call(
        store_kernel,
        out_shape=(
            jax.ShapeDtypeStruct((4, 128), F32),
            jax.ShapeDtypeStruct((4, 4, 672), BF16),
            jax.ShapeDtypeStruct((512, 5376), BF16),
        ),
        in_specs=[vmem, vmem, vmem],
        out_specs=(hbm, hbm, hbm),
        scratch_shapes=[dma((10,))],
        compiler_params=pltpu.CompilerParams(vmem_limit_bytes=2**20),
        name="store",
    )(
        *(
            pltpu.with_memory_space_constraint(v, pltpu.VMEM)
            for v in (loss, grad_hidden, grad_weight)
        )
    )


def solution(mesh):
    in_specs = (P(None, "dp", "section"), P(("dp", "section"), None), P(), P())
    out_specs = (P(), P(None, "dp", "section"), P(("dp", "section"), None))
    return jax.shard_map(
        per_device, mesh=mesh, in_specs=in_specs, out_specs=out_specs, check_vma=False
    )
```

time: 606 us -> 85.6 us (0.14)
  waiting for transfers between devices: 356 us -> 0 us
  blocking collectives: 176 us -> 0 us
  Pallas kernels: 0 us -> 84.7 us
  local copies, waits for them, and re-layouts: 34.2 us -> 0 us
  matrix products: 23 us -> 0 us
  between operations: 14.5 us -> 0.8 us
    unnamed x5 -> x0, waiting for transfers between devices: 269 us -> none
    all_gather x1 -> x0, waiting for transfers between devices: 86.9 us -> none  [per_device(): gathered = lax.all_gather(features, 'dp', axis=1, tiled=True)]
    pallas_call x0 -> x2, Pallas kernels: none -> 84.7 us  [the longest x1 82.2 us: per_device(): pl.pallas_call(kernel, out_shape=(pltpu.VMEM((4, 128), F32), pltpu.VMEM((...]
    psum x1 -> x0, blocking collectives: 73.9 us -> none  [per_device(): summed, picked = lax.psum((local_total, picked_local), ('dp', 'section'))]
    pmax x1 -> x0, blocking collectives: 73.7 us -> none  [per_device(): highest = lax.pmax(local_top, ('dp', 'section'))]
    all_gather x1 -> x0, blocking collectives: 28.4 us -> none  [per_device(): features = lax.all_gather(final_hidden, 'section', axis=2, tiled=True)]
    dot_general x3 -> x0, matrix products: 23 us -> none  [the longest x1 8.38 us: per_device(): jnp.dot(logit_grads, out_weight, preferred_element_type=jnp.float32)]
    unnamed x15 -> x0, local copies, waits for them, and re-layouts: 22.8 us -> none
  transfers between devices with their start and end apart: 3 -> 0, of which waited for: 3 -> 0; matrix products, arithmetic and copies ran while one was open for 1% -> 0% of each run, Pallas kernels for 0% -> 0%
where the time goes in v3:
time: 85.6 us; the launch traced here: 85.5 us
  Pallas kernels  84.7 us (99%)
    pallas_call x1, Pallas kernels, per_device(): pl.pallas_call(kernel, out_shape=(pltpu.VMEM((4, 128), F32), pltpu.VMEM((...  82.2 us
    pallas_call x1, Pallas kernels, per_device(): pl.pallas_call(store_kernel, out_shape=(jax.ShapeDtypeStruct((4, 128), F3...  2.54 us

profile of v3, /device:TPU:8, one launch (start us, length us, event | category | flops | bytes accessed | tf_op | source)
XLA Modules:
  0.0 85.5 jit_solution(11603804275910141914)
XLA Ops:
  0.6 82.2 %xent.1 = (f32[4,128]{1,0:T(4,128)S(1)}, bf16[4,4,672]{2,1,0:T(4,128)(2,1)S(1)}, bf16[512,5376]{1,0:T(8,128)(2,1)S(1)}) custom-call(bf16[4,4,672]{2,1,0:T(4,128)(2,1)} %h_hbm.1, bf16[512,5376]{1,0:T(8,128)(2,1)} %w_hbm.1, s32[4,128]{1,0:T(4,128)} %tgt_hbm.1, f32[4,128]{1,0:T(4,128)} %tw_hbm.1), custom_call_target="tpu_custom_call" | custom-call | tf_op jit(solution)/shard_map/xent/pallas_call | solution.py:651
  82.8 2.5 %store.1 = (f32[4,128]{1,0:T(4,128)}, bf16[4,4,672]{2,1,0:T(4,128)(2,1)}, bf16[512,5376]{1,0:T(8,128)(2,1)}) custom-call(f32[4,128]{1,0:T(4,128)S(1)} %get-tuple-element.6.loss, bf16[4,4,672]{2,1,0:T(4,128)(2,1)S(1)} %get-tuple-element.7.gh, bf16[512,5376]{1,0:T(8,128)(2,1)S(1)} %get-tuple-element.8.gw), custom_call_target="tpu_custom_call" | custom-call | tf_op jit(solution)/shard_map/store/pallas_call | solution.py:666

commit v4 on v3

v4 whole, which is shorter than its diff:
```python
import heapq
import math

import jax
import jax.numpy as jnp
from jax import lax
from jax.experimental import pallas as pl
from jax.experimental.pallas import tpu as pltpu
from jax.sharding import PartitionSpec as P

MESH = pl.DeviceIdType.MESH
F32, BF16 = jnp.float32, jnp.bfloat16
NX, NY, NZ = 4, 4, 8
FRAME = 768
PARTS = 3
LANES = 256
HALVES = 1
TOKENS = 512
REL = (2, 1, 3, 0)
FAR_FIRST = {4: (2, 1, 3), 8: (4, 3, 5, 2, 6, 1, 7)}
SENDS, GROUPS = 4, 71


def frame_tile(section):
    return (21 * section) // 4


def run_by_time(tasks):
    heap = []
    for k, (start, task) in enumerate(tasks):
        heapq.heappush(heap, (start, k, task))
    while heap:
        _, k, task = heapq.heappop(heap)
        try:
            heapq.heappush(heap, (next(task), k, task))
        except StopIteration:
            pass


def pieces(v):
    hi = v.astype(BF16).astype(F32)
    mid = (v - hi).astype(BF16).astype(F32)
    return hi, mid, v - hi - mid


def kernel(
    h_hbm, w_hbm, tgt_hbm, tw_hbm,
    loss_ref, gh_ref, gw,
    h_ref, tgt_ref, tw_ref, h, pt, w, lt, p, pad, mine, rows, tgt, tw,
    a01, a2,
    gs, rc, s0, s1, s2, u0a, u0b, l0, m0, u1a, u1b, l1, m1, l2, m2,
    t0, t1, t2, q0, q1, q2, c0, c1, d0, d1,
    st1, st2,
    in_sem, send_sem, recv_sem,
):
    dp = lax.axis_index("dp")
    section = lax.axis_index("section")
    z, y = dp // NY, dp % NY
    x, c = section // 2, section % 2
    other = 1 - c

    def at(dz=0, dy=0, dx=0, dc=0):
        return (
            lax.rem(z + dz, NZ) * NY + lax.rem(y + dy, NY),
            lax.rem(x + dx, NX) * 2 + lax.rem(c + dc, 2),
        )

    def zo(o):
        return lax.rem(z + o + NZ, NZ)

    def yo(o):
        return lax.rem(y + o + NY, NY)

    def xo(o):
        return lax.rem(x + o + NX, NX)

    sibling = at(dc=1)
    x_right, x_left = at(dx=1), at(dx=3)
    y_right, y_left = at(dy=1), at(dy=3)
    z_right, z_left = at(dz=1), at(dz=7)

    load_h = pltpu.make_async_copy(h_hbm, h_ref, in_sem.at[0])
    load_tgt = pltpu.make_async_copy(tgt_hbm, tgt_ref, in_sem.at[1])
    load_tw = pltpu.make_async_copy(tw_hbm, tw_ref, in_sem.at[2])
    load_w = pltpu.make_async_copy(w_hbm, w, in_sem.at[3])
    for load in (load_h, load_tgt, load_tw):
        load.start()

    def hops(o, n):
        return min(o, n - o)

    plane = [(k // NX, k % NX) for k in range(1, NX * NY)]
    plane.sort(key=lambda d: -hops(d[0], NY) - hops(d[1], NX))
    column = [(k // 2, k % 2) for k in range(1, NZ * 2)]
    column.sort(key=lambda d: -hops(d[0], NZ) - d[1] / 2)
    barrier = pltpu.get_barrier_semaphore()
    for dz, dc in column:
        pl.semaphore_signal(barrier, inc=1, device_id=at(dz=dz, dc=dc), device_id_type=MESH)
    for dy, dx in plane:
        pl.semaphore_signal(barrier, inc=1, device_id=at(dy=dy, dx=dx), device_id_type=MESH)

    rows[...] = jnp.zeros_like(rows)
    pad[...] = jnp.zeros_like(pad)
    st1[...] = jnp.zeros_like(st1)
    st2[...] = jnp.zeros_like(st2)
    load_h.wait()
    for m in range(4):
        pad[4 * m : 4 * m + 4, 0:672] = h_ref[m].astype(F32)
    shift = lax.rem(section, 4) * 32
    framed = pltpu.roll(pad[...], shift, axis=1).astype(BF16)
    a01[0, c, x, z, y] = framed[:, 0:512]
    a2[0, c, x, z, y] = framed[:, 512:768]

    pl.semaphore_wait(barrier, len(plane) + len(column))

    def wait_tiles(sem, tiles, sent):
        r = max(d for d in range(1, 33) if tiles % d == 0 and tiles // d <= 42)
        ref = h.at[pl.ds(0, 16 * r), pl.ds(0, 128 * (tiles // r))]
        copy = pltpu.make_async_remote_copy(
            src_ref=ref, dst_ref=ref, send_sem=sem, recv_sem=sem,
            device_id=sibling, device_id_type=MESH,
        )
        if sent:
            copy.wait_send()
        else:
            copy.wait_recv()

    groups = []
    sends = [0]

    def group():
        groups.append(0)
        return len(groups) - 1

    def send(src, dst, device, g):
        tiles = math.prod(src.shape) * jnp.dtype(src.dtype).itemsize // 4096
        if sends[-1] >= 703 and any(
            sends[-1] % d == 0 and sends[-1] // d <= 42 for d in range(1, 33)
        ):
            sends.append(0)
        groups[g] += tiles
        sends[-1] += tiles
        pltpu.make_async_remote_copy(
            src_ref=src, dst_ref=dst, send_sem=send_sem.at[len(sends) - 1],
            recv_sem=recv_sem.at[g], device_id=device, device_id_type=MESH,
        ).start()

    def arrive(g):
        wait_tiles(recv_sem.at[g], groups[g], False)

    def gather(ref, axis, n):
        g = group()
        for o in FAR_FIRST[n]:
            send(ref, ref, at(**{"d" + axis: o}), g)
        return g

    done = set()

    def finish(name):
        done.add(name)

    from_sibling01 = [group() for _ in range(HALVES)]
    from_sibling2 = [group() for _ in range(HALVES)]

    def gather01(q, t):
        first, second = pl.ds(0, LANES), pl.ds(LANES, LANES)

        def pass_on(ref):
            send(ref, ref, sibling, from_sibling01[q])

        def part0(o, k):
            return a01.at[q, c, xo(o), :, yo(k), :, first]

        def part1(o, k):
            return a01.at[q, c, xo(k), :, yo(o), :, second]

        e = gather(a01.at[q, c, x, z, y], "z", NZ)
        yield t[0]
        arrive(e)
        e0 = gather(a01.at[q, c, x, :, y, :, first], "y", NY)
        e1 = gather(a01.at[q, c, x, :, y, :, second], "x", NX)
        zero0, zero1 = group(), group()
        for part, right, left, zero in (
            (part0, x_right, x_left, zero0), (part1, y_right, y_left, zero1)
        ):
            send(part(0, 0), part(0, 0), right, zero)
            send(part(0, 0), part(0, 0), left, zero)
        yield t[1]
        rings = []
        for e, part, right, left, zero in (
            (e0, part0, x_right, x_left, zero0), (e1, part1, y_right, y_left, zero1)
        ):
            arrive(e)
            near, far, last = group(), group(), group()
            rings.append((part, right, left, near, far, last, zero))
            send(part(0, 1), part(0, 1), right, near)
            send(part(0, 3), part(0, 3), left, near)
            send(part(0, 2), part(0, 2), left, far)
            send(part(0, 2), part(0, 2), right, far)
            send(part(0, 3), part(0, 3), right, far)
            send(part(0, 1), part(0, 1), left, far)
        for part, right, left, near, far, last, zero in rings:
            arrive(zero)
            send(part(-1, 0), part(-1, 0), right, last)
        pass_on(a01.at[q, c, x, :, :, :, first])
        pass_on(a01.at[q, c, :, :, y, :, second])
        yield t[2]
        for part, right, left, near, far, last, zero in rings:
            arrive(near)
            send(part(-1, 1), part(-1, 1), right, last)
            send(part(1, 3), part(1, 3), left, last)
        yield t[3]
        for part, right, left, near, far, last, zero in rings:
            arrive(far)
            send(part(1, 2), part(1, 2), left, last)
        pass_on(a01.at[q, c, xo(-1), :, :, :, first])
        pass_on(a01.at[q, c, xo(1), :, :, :, first])
        pass_on(a01.at[q, c, :, :, yo(-1), :, second])
        pass_on(a01.at[q, c, :, :, yo(1), :, second])
        yield t[4]
        arrive(rings[0][5])
        pass_on(a01.at[q, c, xo(2), :, :, :, first])
        arrive(rings[1][5])
        pass_on(a01.at[q, c, :, :, yo(2), :, second])
        finish(("gather01", q))

    def gather2(q, t):
        def pass_on(ref):
            send(ref, ref, sibling, from_sibling2[q])

        def part(o, i):
            return a2.at[q, c, :, zo(o), yo(i)]

        e = gather(a2.at[q, c, x, z, y], "x", NX)
        yield t[0]
        arrive(e)
        e = gather(a2.at[q, c, :, z, y], "y", NY)
        hop = [group() for _ in range(NY)]
        send(part(0, 0), part(0, 0), z_right, hop[0])
        send(part(0, 0), part(0, 0), z_left, hop[0])
        yield t[1]
        arrive(e)
        for i in (1, 2, 3):
            send(part(0, i), part(0, i), z_right, hop[i])
            send(part(0, i), part(0, i), z_left, hop[i])
        pass_on(a2.at[q, c, :, z])
        for o in (1, 2, 3):
            after = [group() for _ in range(NY)] if o < 3 else [group()] * NY
            for i in range(NY):
                yield t[1] + o * t[2] + i * 0.7 - 0.7
                arrive(hop[i])
                if o < 3 or i < 2:
                    send(part(-o, i), part(-o, i), z_right, after[i])
                if o < 3 or i >= 2:
                    send(part(o, i), part(o, i), z_left, after[i])
            hop = after
            pass_on(a2.at[q, c, :, zo(-o)])
            pass_on(a2.at[q, c, :, zo(o)])
        yield t[1] + 4 * t[2]
        arrive(hop[0])
        pass_on(a2.at[q, c, :, zo(4)])
        finish(("gather2", q))

    def token_order():
        load_w.start()
        yield 1.0
        load_tgt.wait()
        load_tw.wait()
        t = tgt_ref[...]
        parts = [(t & 63).astype(F32), ((t >> 6) & 63).astype(F32), (t >> 12).astype(F32)]
        parts += list(pieces(tw_ref[...]))
        for i in range(6):
            for m in range(4):
                rows[m, i : i + 1, :] = parts[i][m : m + 1, :]
        src = lax.broadcasted_iota(jnp.int32, (128, 512), 0)
        dst = lax.broadcasted_iota(jnp.int32, (128, 512), 1)
        out = jnp.zeros((8, 512), F32)
        for m in range(4):
            hot = dst == (src // 4) * 16 + m * 4 + src % 4
            out += jnp.dot(
                rows[m].astype(BF16), hot.astype(BF16), preferred_element_type=F32
            )
        number = out[0:1].astype(jnp.int32) + out[1:2].astype(jnp.int32) * 64
        tgt[...] = number + out[2:3].astype(jnp.int32) * 4096
        tw[...] = out[3:4] + out[4:5] + out[5:6]

    first_id = (dp * (NX * 2) + section) * 512

    def combine(buf):
        v = buf[...]
        m = jnp.max(v[:, 0:4], axis=0)
        total = m + jnp.log(jnp.sum(jnp.exp(v[:, 0:4] - m[None]), axis=0))
        return total, jnp.sum(v[:, 4:8], axis=0)

    def frame_part(q, s, tile, zz):
        lane = tile * 128
        if tile < 4:
            v = a01[q, s % 2, s // 2, zz, :, :, lane : lane + 128]
        else:
            v = a2[q, s % 2, s // 2, zz, :, :, lane - 512 : lane - 384]
        return v.reshape(NY * 16, 128)

    def assemble(q, first, last):
        def step(zz, carry):
            dst = pl.ds(pl.multiple_of(zz * 64, 64), 64)
            for tile in range(42):
                v = None
                for s in range(8):
                    if frame_tile(s) <= tile < frame_tile(s) + 6:
                        part = frame_part(q, s, tile - frame_tile(s), zz)
                        v = part if v is None else v + part
                h[dst, tile * 128 : tile * 128 + 128] = v
            return carry

        lax.fori_loop(first, last, step, 0)

    def loss_order(q, loss):
        for i, v in enumerate(pieces(loss)):
            rows[i] = jnp.concatenate([v, jnp.zeros((4, 128), F32)], axis=0)
        src = lax.broadcasted_iota(jnp.int32, (128, 128), 0)
        dst = lax.broadcasted_iota(jnp.int32, (128, 128), 1)
        pick = lax.broadcasted_iota(jnp.int32, (8, 128), 0) == (
            lax.broadcasted_iota(jnp.int32, (8, 128), 1) // 32
        )
        for m in range(4):
            hot = (src == ((dst // 4) % 8) * 16 + m * 4 + dst % 4).astype(BF16)
            v = sum(
                jnp.dot(rows[i].astype(BF16), hot, preferred_element_type=F32)
                for i in range(3)
            )
            loss_ref[m : m + 1, :] = jnp.sum(jnp.where(pick, v, 0.0), axis=0, keepdims=True)

    def share(q, s):
        cols = pl.ds(pl.multiple_of(frame_tile(s) * 128, 128), FRAME)
        return lax.dot_general(
            p[q], w[:, cols], (((1,), (0,)), ((), ())), preferred_element_type=F32
        )

    up, down = pl.ds(0, 4), pl.ds(4, 4)
    up_slice, down_slice = slice(0, 4), slice(4, 8)
    front, back = pl.ds(0, 2), pl.ds(2, 2)
    near0, near1, far0, far1 = ([group() for _ in range(HALVES)] for _ in range(4))
    to_right, to_left = (0, 3), (1, 2)
    ring_r = [
        {(k, i): group() for k in (1, 2, 3, 4) for i in range(NX) if k > 1 or i in to_right}
        for _ in range(HALVES)
    ]
    ring_l = [
        {(k, i): group() for k in (1, 2, 3, 4) for i in range(NX) if k > 1 or i in to_left}
        for _ in range(HALVES)
    ]
    tasks = []

    def main(q, t):
        cols = slice(q * TOKENS, q * TOKENS + TOKENS)
        yield t[0]
        assert ("gather01", q) in done and ("gather2", q) in done
        load_w.wait()
        for parity in (c, other):
            if parity is other:
                arrive(from_sibling01[q])
                arrive(from_sibling2[q])
            for xx in range(NX):
                acc = None
                for buf, off, lane in ((a01, 0, 0), (a01, 256, 256), (a2, 0, 512)):
                    feats = frame_tile(2 * xx + parity) * 128 + lane
                    rows_s = buf[q, parity, xx, :, :, :, off : off + LANES]
                    v = lax.dot_general(
                        w[:, pl.ds(pl.multiple_of(feats, 128), LANES)],
                        rows_s.reshape(TOKENS, LANES),
                        (((1,), (1,)), ((), ())), preferred_element_type=F32,
                    )
                    acc = v if acc is None else acc + v
                if parity is c and xx == 0:
                    lt[q] = acc
                else:
                    lt[q] += acc
        ids = first_id + lax.broadcasted_iota(jnp.int32, (512, TOKENS), 0)
        logits = lt[q]
        picked = jnp.sum(jnp.where(ids == tgt[:, cols], logits, 0.0), axis=0, keepdims=True)
        top = jnp.max(logits, axis=0, keepdims=True)
        lse = top + jnp.log(jnp.sum(jnp.exp(logits - top), axis=0, keepdims=True))
        for i in range(4):
            st1[q, 0, i : i + 1, :] = lse[:, i * 128 : i * 128 + 128]
            st1[q, 0, 4 + i : 5 + i, :] = picked[:, i * 128 : i * 128 + 128]
        around = group()
        for k, d in enumerate(plane):
            send(st1.at[q, 0], st1.at[q, k + 1], at(dy=d[0], dx=d[1]), around)
        assemble(q, 0, 4)
        yield t[1]
        arrive(around)
        total, hit = combine(st1.at[q])
        st2[q, 0, 0:4, :] = total
        st2[q, 0, 4:8, :] = hit
        around = group()
        for k, d in enumerate(column):
            send(st2.at[q, 0], st2.at[q, k + 1], at(dz=d[0], dc=d[1]), around)
        assemble(q, 4, 8)
        yield t[2]
        arrive(around)
        log_norm, hit = combine(st2.at[q])
        norm_row = jnp.concatenate([log_norm[i : i + 1] for i in range(4)], axis=1)
        for b in range(4):
            r = slice(b * 128, b * 128 + 128)
            ids = first_id + b * 128 + lax.broadcasted_iota(jnp.int32, (128, TOKENS), 0)
            hot = (ids == tgt[:, cols]).astype(F32)
            g = tw[:, cols] * (jnp.exp(lt[q, r, :] - norm_row) - hot)
            pt[r, cols] = g.astype(BF16)
            p[q, :, r] = jnp.transpose(g).astype(BF16)
        core = []
        for i, o in enumerate(REL):
            gs[q, i] = share(q, xo(o) * 2 + other).astype(BF16)
            core.append(group())
            send(gs.at[q, i], rc.at[q, i], sibling, core[i])
        for i in range(NX):
            yield t[3] + i * 0.7
            mine[...] = share(q, xo(REL[i]) * 2 + c)
            arrive(core[i])
            for zz in range(NZ):
                r = slice(zz * 64, zz * 64 + 64)
                v = (mine[r, :] + rc[q, i, r, :].astype(F32)).astype(BF16)
                s0[q, i, zz] = v[:, 0:256].reshape(NY, 16, LANES)
                for yy in range(NY):
                    s1[q, yy, i, zz] = v[yy * 16 : yy * 16 + 16, 256:512]
                s2[q, zz, i] = v[:, 512:768].reshape(NY, 16, LANES)
            first_sends(q, i)
        loss_order(q, log_norm - hit)
        finish(("main", q))

    def first_sends(q, i):
        if i == 0:
            send(s0.at[q, 0, up], u0a.at[q], x_right, near0[q])
            send(s0.at[q, 0, down], u0b.at[q], x_left, near0[q])
        if i in to_right:
            send(s2.at[q, zo(4), i], l2.at[q, 0, i], z_right, ring_r[q][1, i])
            send(s2.at[q, zo(-3), i], m2.at[q, 1, i], z_left, ring_l[q][2, i])
        else:
            send(s2.at[q, zo(4), i], m2.at[q, 0, i], z_left, ring_l[q][1, i])
            send(s2.at[q, zo(3), i], l2.at[q, 1, i], z_right, ring_r[q][2, i])
        if i == 1:
            send(s1.at[q, yo(2), front], u1a.at[q], y_right, near1[q])
            send(s1.at[q, yo(-1), front], m1.at[q, front], y_left, far1[q])
            send(s0.at[q, 1, down], l0.at[q, down], x_right, far0[q])
        if i == 2:
            send(s0.at[q, 2, up], m0.at[q, up], x_left, far0[q])
        if i == 3:
            send(s1.at[q, yo(2), back], u1b.at[q], y_left, near1[q])
            send(s1.at[q, yo(1), back], l1.at[q, back], y_right, far1[q])

    def scatter0(q, t):
        yield t[0]
        arrive(near0[q])
        s0[q, 1, up_slice] = (
            s0[q, 1, up_slice].astype(F32) + u0a[q].astype(F32)
        ).astype(BF16)
        send(s0.at[q, 1, up], l0.at[q, up], x_right, far0[q])
        s0[q, 2, down_slice] = (
            s0[q, 2, down_slice].astype(F32) + u0b[q].astype(F32)
        ).astype(BF16)
        send(s0.at[q, 2, down], m0.at[q, down], x_left, far0[q])
        yield t[1]
        assert ("main", q) in done
        arrive(far0[q])
        for zz in range(NZ):
            v = s0[q, 3, zz].astype(F32) + l0[q, zz].astype(F32) + m0[q, zz].astype(F32)
            v = v.astype(BF16)
            for yy in range(NY):
                t0[q, yy, zz] = v[yy]
        e = group()
        for o in FAR_FIRST[NY]:
            send(t0.at[q, yo(o)], q0.at[q, o - 1], at(dy=o), e)
        yield t[2]
        arrive(e)
        v = sum([q0[q, k].astype(F32) for k in range(NY - 1)], t0[q, y].astype(F32))
        c0[q] = v.astype(BF16)
        e = group()
        for o in FAR_FIRST[NZ]:
            send(c0.at[q, zo(o)], d0.at[q, o - 1], at(dz=o), e)
        yield t[3]
        arrive(e)
        pad[:, 0:256] = sum(
            [d0[q, k].astype(F32) for k in range(NZ - 1)], c0[q, z].astype(F32)
        )
        finish(("scatter0", q))
        write_hidden(q)

    def scatter1(q, t):
        yield t[0]
        assert ("main", q) in done
        arrive(near1[q])
        r = yo(1)
        s1[q, r, 0:2] = (s1[q, r, 0:2].astype(F32) + u1a[q].astype(F32)).astype(BF16)
        send(s1.at[q, r, front], l1.at[q, front], y_right, far1[q])
        r = yo(-1)
        s1[q, r, 2:4] = (s1[q, r, 2:4].astype(F32) + u1b[q].astype(F32)).astype(BF16)
        send(s1.at[q, r, back], m1.at[q, back], y_left, far1[q])
        yield t[1]
        arrive(far1[q])
        e = group()
        for i, o in enumerate(REL):
            v = s1[q, y, i].astype(F32) + l1[q, i].astype(F32) + m1[q, i].astype(F32)
            t1[q, i] = v.astype(BF16)
            if o:
                send(t1.at[q, i], q1.at[q, o - 1], at(dx=o), e)
        yield t[2]
        arrive(e)
        v = sum([q1[q, k].astype(F32) for k in range(NX - 1)], t1[q, 3].astype(F32))
        c1[q] = v.astype(BF16)
        e = group()
        for o in FAR_FIRST[NZ]:
            send(c1.at[q, zo(o)], d1.at[q, o - 1], at(dz=o), e)
        yield t[3]
        arrive(e)
        pad[:, 256:512] = sum(
            [d1[q, k].astype(F32) for k in range(NZ - 1)], c1[q, z].astype(F32)
        )
        finish(("scatter1", q))
        write_hidden(q)

    def scatter2(q, t, i, moving_right):
        ring = (ring_r if moving_right else ring_l)[q]
        got = l2 if moving_right else m2
        to = z_right if moving_right else z_left
        for k in (1, 2, 3):
            yield t[k - 1]
            if (k, i) not in ring:
                continue
            arrive(ring[k, i])
            r = zo(4 - k) if moving_right else zo(k - 4)
            v = s2[q, r, i].astype(F32) + got[q, k - 1, i].astype(F32)
            s2[q, r, i] = v.astype(BF16)
            send(s2.at[q, r, i], got.at[q, k, i], to, ring[k + 1, i])
        finish(("ring2", i, moving_right))

    def scatter2_end(q, t):
        yield t[0]
        e = group()
        for i in range(NX):
            assert ("ring2", i, True) in done and ("ring2", i, False) in done
            arrive(ring_r[q][4, i])
            arrive(ring_l[q][4, i])
            v = s2[q, z, i].astype(F32) + l2[q, 3, i].astype(F32) + m2[q, 3, i].astype(F32)
            t2[q, i] = v.astype(BF16)
        for k, (dy, dx) in enumerate(plane):
            send(t2.at[q, REL.index(dx), yo(dy)], q2.at[q, k], at(dy=dy, dx=dx), e)
        yield t[1]
        arrive(e)
        pad[:, 512:768] = sum(
            [q2[q, k].astype(F32) for k in range(len(plane))], t2[q, 3, y].astype(F32)
        )
        finish(("scatter2", q))
        write_hidden(q)

    def write_hidden(q):
        if all((name, q) in done for name in ("scatter0", "scatter1", "scatter2")):
            pad[...] = pltpu.roll(pad[...], lax.rem(FRAME - shift, FRAME), axis=1)
            for m in range(4):
                gh_ref[m] = pad[4 * m : 4 * m + 4, 0:672].astype(BF16)

    def weight(t):
        for k in range(14):
            yield t + 0.6 * k
            assert ("main", 0) in done
            feats = slice(k * 384, k * 384 + 384)
            gw[:, feats] = lax.dot_general(
                pt[...], h[:, feats], (((1,), (0,)), ((), ())), preferred_element_type=F32
            ).astype(BF16)

    run_by_time(
        [
            (0.0, gather01(0, (6.0, 10.3, 13.3, 16.3, 19.3))),
            (0.1, gather2(0, (2.6, 6.0, 3.4))),
            (0.9, token_order()),
            (20.0, main(0, (20.0, 27.0, 32.0, 34.0))),
            (39.0, scatter0(0, (39.0, 44.0, 48.5, 53.5))),
            (43.5, scatter1(0, (43.5, 46.7, 51.5, 56.5))),
            (39.1, scatter2(0, (39.1, 41.5, 43.8), 0, True)),
            (41.4, scatter2(0, (41.4, 41.4, 43.7), 0, False)),
            (40.5, scatter2(0, (40.5, 40.5, 42.9), 1, True)),
            (40.6, scatter2(0, (40.6, 42.8, 45.0), 1, False)),
            (42.0, scatter2(0, (42.0, 42.0, 44.3), 2, True)),
            (42.1, scatter2(0, (42.1, 44.4, 46.7), 2, False)),
            (43.3, scatter2(0, (43.3, 45.5, 47.7), 3, True)),
            (43.4, scatter2(0, (43.4, 43.4, 45.6), 3, False)),
            (50.5, scatter2_end(0, (50.5, 55.5))),
            (46.0, weight(46.0)),
        ]
    )

    for k, tiles in enumerate(sends):
        wait_tiles(send_sem.at[k], tiles, True)
    assert len(sends) == SENDS and len(groups) == GROUPS, (len(sends), len(groups))


def store_kernel(loss, gh, gw, loss_out, gh_out, gw_out, sem):
    copies = [
        pltpu.make_async_copy(loss, loss_out, sem.at[8]),
        pltpu.make_async_copy(gh, gh_out, sem.at[9]),
    ]
    for k in range(8):
        r = pl.ds(64 * k, 64)
        copies.append(pltpu.make_async_copy(gw.at[r], gw_out.at[r], sem.at[k]))
    for copy in copies:
        copy.start()
    for copy in copies:
        copy.wait()


def per_device(final_hidden, out_weight, targets, token_weight):
    vm, dma = pltpu.VMEM, pltpu.SemaphoreType.DMA
    n = HALVES
    scratch = [
        vm((4, 4, 672), BF16),
        vm((4, 128), jnp.int32),
        vm((4, 128), F32),
        vm((512, 5376), BF16),
        vm((512, 512), BF16),
        vm((512, 5376), BF16),
        vm((n, 512, TOKENS), F32),
        vm((n, TOKENS, 512), BF16),
        vm((16, FRAME), F32),
        vm((TOKENS, FRAME), F32),
        vm((4, 8, 128), F32),
        vm((1, 512), jnp.int32),
        vm((1, 512), F32),
        vm((n, 2, NX, NZ, NY, 16, 2 * LANES), BF16),
        vm((n, 2, NX, NZ, NY, 16, LANES), BF16),
        vm((n, NX, TOKENS, FRAME), BF16),
        vm((n, NX, TOKENS, FRAME), BF16),
        vm((n, NX, NZ, NY, 16, LANES), BF16),
        vm((n, NY, NX, NZ, 16, LANES), BF16),
        vm((n, NZ, NX, NY, 16, LANES), BF16),
        vm((n, 4, NY, 16, LANES), BF16),
        vm((n, 4, NY, 16, LANES), BF16),
        vm((n, NZ, NY, 16, LANES), BF16),
        vm((n, NZ, NY, 16, LANES), BF16),
        vm((n, 2, NZ, 16, LANES), BF16),
        vm((n, 2, NZ, 16, LANES), BF16),
        vm((n, NX, NZ, 16, LANES), BF16),
        vm((n, NX, NZ, 16, LANES), BF16),
        vm((n, 4, NX, NY, 16, LANES), BF16),
        vm((n, 4, NX, NY, 16, LANES), BF16),
        vm((n, NY, NZ, 16, LANES), BF16),
        vm((n, NX, NZ, 16, LANES), BF16),
        vm((n, NX, NY, 16, LANES), BF16),
        vm((n, NY - 1, NZ, 16, LANES), BF16),
        vm((n, NX - 1, NZ, 16, LANES), BF16),
        vm((n, NX * NY - 1, 16, LANES), BF16),
        vm((n, NZ, 16, LANES), BF16),
        vm((n, NZ, 16, LANES), BF16),
        vm((n, NZ - 1, 16, LANES), BF16),
        vm((n, NZ - 1, 16, LANES), BF16),
        vm((n, 16, 8, 128), F32),
        vm((n, 16, 8, 128), F32),
        dma((4,)), dma((SENDS,)), dma((GROUPS,)),
    ]
    vmem = pl.BlockSpec(memory_space=pltpu.VMEM)
    hbm = pl.BlockSpec(memory_space=pl.ANY)
    final_hidden, targets, token_weight = (
        pltpu.with_memory_space_constraint(v, pltpu.HBM)
        for v in (final_hidden, targets, token_weight)
    )
    loss, grad_hidden, grad_weight = pl.pallas_call(
        kernel,
        out_shape=(
            pltpu.VMEM((4, 128), F32),
            pltpu.VMEM((4, 4, 672), BF16),
            pltpu.VMEM((512, 5376), BF16),
        ),
        in_specs=[hbm, hbm, hbm, hbm],
        out_specs=(vmem, vmem, vmem),
        scratch_shapes=scratch,
        compiler_params=pltpu.CompilerParams(
            collective_id=0, has_side_effects=True, vmem_limit_bytes=48 * 2**20
        ),
        name="xent",
    )(final_hidden, out_weight, targets, token_weight)
    return pl.pallas_call(
        store_kernel,
        out_shape=(
            jax.ShapeDtypeStruct((4, 128), F32),
            jax.ShapeDtypeStruct((4, 4, 672), BF16),
            jax.ShapeDtypeStruct((512, 5376), BF16),
        ),
        in_specs=[vmem, vmem, vmem],
        out_specs=(hbm, hbm, hbm),
        scratch_shapes=[dma((10,))],
        compiler_params=pltpu.CompilerParams(vmem_limit_bytes=2**20),
        name="store",
    )(
        *(
            pltpu.with_memory_space_constraint(v, pltpu.VMEM)
            for v in (loss, grad_hidden, grad_weight)
        )
    )


def solution(mesh):
    in_specs = (P(None, "dp", "section"), P(("dp", "section"), None), P(), P())
    out_specs = (P(), P(None, "dp", "section"), P(("dp", "section"), None))
    return jax.shard_map(
        per_device, mesh=mesh, in_specs=in_specs, out_specs=out_specs, check_vma=False
    )
```

time: 85.6 us -> 80.1 us (0.936)
  Pallas kernels: 84.7 us -> 78.7 us
    pallas_call x1, Pallas kernels: 82.2 us -> 76.2 us  [per_device(): pl.pallas_call(kernel, out_shape=(pltpu.VMEM((4, 128), F32), pltpu.VMEM((...]
where the time goes in v4:
time: 80.1 us; the launch traced here: 79.5 us
  Pallas kernels  78.7 us (98%)
    pallas_call x1, Pallas kernels, per_device(): pl.pallas_call(kernel, out_shape=(pltpu.VMEM((4, 128), F32), pltpu.VMEM((...  76.2 us
    pallas_call x1, Pallas kernels, per_device(): pl.pallas_call(store_kernel, out_shape=(jax.ShapeDtypeStruct((4, 128), F3...  2.54 us

profile of v4, /device:TPU:8, one launch (start us, length us, event | category | flops | bytes accessed | tf_op | source)
XLA Modules:
  0.0 79.5 jit_solution(9874882215578306590)
XLA Ops:
  0.6 76.2 %xent.1 = (f32[4,128]{1,0:T(4,128)S(1)}, bf16[4,4,672]{2,1,0:T(4,128)(2,1)S(1)}, bf16[512,5376]{1,0:T(8,128)(2,1)S(1)}) custom-call(bf16[4,4,672]{2,1,0:T(4,128)(2,1)} %h_hbm.1, bf16[512,5376]{1,0:T(8,128)(2,1)} %w_hbm.1, s32[4,128]{1,0:T(4,128)} %tgt_hbm.1, f32[4,128]{1,0:T(4,128)} %tw_hbm.1), custom_call_target="tpu_custom_call" | custom-call | tf_op jit(solution)/shard_map/xent/pallas_call | solution.py:663
  76.8 2.5 %store.1 = (f32[4,128]{1,0:T(4,128)}, bf16[4,4,672]{2,1,0:T(4,128)(2,1)}, bf16[512,5376]{1,0:T(8,128)(2,1)}) custom-call(f32[4,128]{1,0:T(4,128)S(1)} %get-tuple-element.6.loss, bf16[4,4,672]{2,1,0:T(4,128)(2,1)S(1)} %get-tuple-element.7.gh, bf16[512,5376]{1,0:T(8,128)(2,1)S(1)} %get-tuple-element.8.gw), custom_call_target="tpu_custom_call" | custom-call | tf_op jit(solution)/shard_map/store/pallas_call | solution.py:678

commit v5 on v4

--- a/solution.py
+++ b/solution.py
@@ -80,11 +80,7 @@
     z_right, z_left = at(dz=1), at(dz=7)
 
     load_h = pltpu.make_async_copy(h_hbm, h_ref, in_sem.at[0])
-    load_tgt = pltpu.make_async_copy(tgt_hbm, tgt_ref, in_sem.at[1])
-    load_tw = pltpu.make_async_copy(tw_hbm, tw_ref, in_sem.at[2])
-    load_w = pltpu.make_async_copy(w_hbm, w, in_sem.at[3])
-    for load in (load_h, load_tgt, load_tw):
-        load.start()
+    load_h.start()
 
     def hops(o, n):
         return min(o, n - o)
@@ -99,10 +95,14 @@
     for dy, dx in plane:
         pl.semaphore_signal(barrier, inc=1, device_id=at(dy=dy, dx=dx), device_id_type=MESH)
 
+    load_tgt = pltpu.make_async_copy(tgt_hbm, tgt_ref, in_sem.at[1])
+    load_tw = pltpu.make_async_copy(tw_hbm, tw_ref, in_sem.at[2])
+    load_w = pltpu.make_async_copy(w_hbm, w, in_sem.at[3])
+    for load in (load_tgt, load_tw):
+        load.start()
+
     rows[...] = jnp.zeros_like(rows)
     pad[...] = jnp.zeros_like(pad)
-    st1[...] = jnp.zeros_like(st1)
-    st2[...] = jnp.zeros_like(st2)
     load_h.wait()
     for m in range(4):
         pad[4 * m : 4 * m + 4, 0:672] = h_ref[m].astype(F32)
@@ -349,7 +349,7 @@
         {(k, i): group() for k in (1, 2, 3, 4) for i in range(NX) if k > 1 or i in to_left}
         for _ in range(HALVES)
     ]
-    tasks = []
+    side = {}
 
     def main(q, t):
         cols = slice(q * TOKENS, q * TOKENS + TOKENS)
@@ -424,7 +424,7 @@
                     s1[q, yy, i, zz] = v[yy * 16 : yy * 16 + 16, 256:512]
                 s2[q, zz, i] = v[:, 512:768].reshape(NY, 16, LANES)
             first_sends(q, i)
-        loss_order(q, log_norm - hit)
+        side["loss"] = log_norm - hit
         finish(("main", q))
 
     def first_sends(q, i):
@@ -557,9 +557,13 @@
             for m in range(4):
                 gh_ref[m] = pad[4 * m : 4 * m + 4, 0:672].astype(BF16)
 
+    def write_loss(t):
+        yield t
+        loss_order(0, side["loss"])
+
     def weight(t):
         for k in range(14):
-            yield t + 0.6 * k
+            yield t + 0.5 * k
             assert ("main", 0) in done
             feats = slice(k * 384, k * 384 + 384)
             gw[:, feats] = lax.dot_general(
@@ -568,8 +572,8 @@
 
     run_by_time(
         [
-            (0.0, gather01(0, (6.0, 10.3, 13.3, 16.3, 19.3))),
-            (0.1, gather2(0, (2.6, 6.0, 3.4))),
+            (0.05, gather01(0, (6.0, 10.3, 13.3, 16.3, 19.3))),
+            (0.0, gather2(0, (2.6, 6.0, 3.4))),
             (0.9, token_order()),
             (20.0, main(0, (20.0, 27.0, 32.0, 34.0))),
             (39.0, scatter0(0, (39.0, 44.0, 48.5, 53.5))),
@@ -583,7 +587,8 @@
             (43.3, scatter2(0, (43.3, 45.5, 47.7), 3, True)),
             (43.4, scatter2(0, (43.4, 43.4, 45.6), 3, False)),
             (50.5, scatter2_end(0, (50.5, 55.5))),
-            (46.0, weight(46.0)),
+            (48.6, weight(48.6)),
+            (48.7, write_loss(48.7)),
         ]
     )
 

time: 80.1 us -> 80 us (level)
  no operation moved by 1% of the time
where the time goes in v5:
time: 80 us; the launch traced here: 79.7 us
  Pallas kernels  78.9 us (99%)
  between operations  0.8 us (1%)
    pallas_call x1, Pallas kernels, per_device(): pl.pallas_call(kernel, out_shape=(pltpu.VMEM((4, 128), F32), pltpu.VMEM((...  76.3 us
    pallas_call x1, Pallas kernels, per_device(): pl.pallas_call(store_kernel, out_shape=(jax.ShapeDtypeStruct((4, 128), F3...  2.54 us

profile of v5, /device:TPU:8, one launch (start us, length us, event | category | flops | bytes accessed | tf_op | source)
XLA Modules:
  0.0 79.7 jit_solution(10494507044223545992)
XLA Ops:
  0.6 76.3 %xent.1 = (f32[4,128]{1,0:T(4,128)S(1)}, bf16[4,4,672]{2,1,0:T(4,128)(2,1)S(1)}, bf16[512,5376]{1,0:T(8,128)(2,1)S(1)}) custom-call(bf16[4,4,672]{2,1,0:T(4,128)(2,1)} %h_hbm.1, bf16[512,5376]{1,0:T(8,128)(2,1)} %w_hbm.1, s32[4,128]{1,0:T(4,128)} %tgt_hbm.1, f32[4,128]{1,0:T(4,128)} %tw_hbm.1), custom_call_target="tpu_custom_call" | custom-call | tf_op jit(solution)/shard_map/xent/pallas_call | solution.py:668
  77.0 2.5 %store.1 = (f32[4,128]{1,0:T(4,128)}, bf16[4,4,672]{2,1,0:T(4,128)(2,1)}, bf16[512,5376]{1,0:T(8,128)(2,1)}) custom-call(f32[4,128]{1,0:T(4,128)S(1)} %get-tuple-element.6.loss, bf16[4,4,672]{2,1,0:T(4,128)(2,1)S(1)} %get-tuple-element.7.gh, bf16[512,5376]{1,0:T(8,128)(2,1)S(1)} %get-tuple-element.8.gw), custom_call_target="tpu_custom_call" | custom-call | tf_op jit(solution)/shard_map/store/pallas_call | solution.py:683
